TPU v7x, 32 devices: a whole 2x2x4 slice. The times are simulated.
32 devices in a mesh: scan: 4 (over y, core), ybrick: 8 (over z, x).
Axes of the slice: x: 2, y: 2, z: 4, core: 2. Of those that a mesh axis runs over, the one named last changes fastest.
Arguments:
- raw: bfloat16 [16, 1024, 2048], P(None, 'ybrick', 'scan'), may hold values from 0.099609375 to 4
- row_shift: int32 [16], replicated, may hold values from 0 to 255
- frac_index: int32 [16], replicated, may hold values from 0 to 15
- psf_y: float32 [65], replicated, may hold values from 0.05 to 1
- psf_x: float32 [65], replicated, may hold values from 0.05 to 1
Outputs:
- estimate: float32 [16, 1024, 2048], P('scan', 'ybrick')
All inputs are finite; a program needn't handle non-finite values.
Results may differ from a plain program's by a relative error of at most 0.0021.
Values may be sent and summed in bfloat16 or wider, within the bound.
No kernel may reach another device: no remote copies, remote signals or barrier semaphores. Data moves between devices by JAX's collectives and lax.ppermute only.
A program may use at most 128 MiB of HBM per device.

v0:
```python
import functools

import jax
import jax.numpy as jnp
from jax import lax
from jax.experimental import pallas as pl
from jax.experimental.pallas import tpu as pltpu
from jax.sharding import PartitionSpec as P

RADIUS = 32
ITERS = 2
NFRAC = 16
BACKGROUND = 0.5

HALO = 2 * ITERS * RADIUS
ROWS = 192
COLS = 256
MARGIN = 128
ALIGN = 16
TINY = 1e-30
VMEM_BYTES = 32 * 2**20


def shifted_2(x, axis, by):
    devices = lax.axis_size(axis)
    pairs = [(i, i + by) for i in range(devices) if 0 <= i + by < devices]
    return lax.ppermute(x, axis, pairs)


def with_halo(x, sides, width):
    for axis, dim in sides:
        devices, length = (lax.axis_size(axis), x.shape[dim])
        up = [(i, (i + 1) % devices) for i in range(devices - 1)]
        down = [(j, i) for i, j in up]
        last = lax.slice_in_dim(x, length - width, length, axis=dim)
        initial = lax.slice_in_dim(x, 0, width, axis=dim)
        before = lax.ppermute(last, axis, up)
        after = lax.ppermute(initial, axis, down)
        x = jnp.concatenate([before, x, after], axis=dim)
    return x


def band_matrix(kernel, count_in, count_out, offset):
    inputs = jnp.arange(count_in, dtype=jnp.int32)[:, None]
    outputs = jnp.arange(count_out, dtype=jnp.int32)[None, :]
    onehot = jax.nn.one_hot(inputs - outputs + offset, kernel.shape[0], dtype=jnp.float32)
    return jnp.dot(onehot, kernel, precision=lax.Precision.HIGHEST)


def along_rows(source, matrix):
    return jnp.einsum("io,pix->pox", matrix, source, precision=lax.Precision.HIGHEST)


def along_columns(source, matrix):

    def per_frame(frame_data):
        height, width = frame_data.shape
        padded = jnp.pad(frame_data, ((0, 0), (128, 128)))
        blocks = padded.reshape(height, width // 128 + 2, 128)
        windows = jnp.concatenate([blocks[:, :-2], blocks[:, 1:-1], blocks[:, 2:]], axis=-1)
        return jnp.einsum("rbi,io->rbo", windows, matrix, precision=lax.Precision.HIGHEST).reshape(
            height, width
        )

    return lax.map(per_frame, source)


def step_bricks(moved, whole_bricks, power):
    shifted = shifted_2(moved, "ybrick", 2**power)
    taken = (whole_bricks // 2**power % 2 == 1)[:, None, None]
    return jnp.where(taken, shifted, moved)


def deskew_brick(stacked, rest, fraction, brick):
    weight = fraction.astype(jnp.float32) / NFRAC
    upper = lax.dynamic_slice_in_dim(stacked, brick - rest, brick, 0)
    lower = lax.dynamic_slice_in_dim(stacked, brick - rest - 1, brick, 0)
    return ((1.0 - weight) * upper + weight * lower).astype(jnp.bfloat16)


def by_bricks(raw, row_shift, frac_index, psf_y, psf_x):
    arranged = lax.all_to_all(raw, "scan", split_axis=0, concat_axis=2, tiled=True)
    group_planes = arranged.shape[0]
    brick = arranged.shape[1]
    first_plane = lax.axis_index("scan") * group_planes
    shifts = lax.dynamic_slice_in_dim(row_shift, first_plane, group_planes)
    fractions = lax.dynamic_slice_in_dim(frac_index, first_plane, group_planes)
    whole_bricks = shifts // brick
    rests = shifts % brick
    moved = arranged
    for power in range((lax.axis_size("ybrick") // 4 - 1).bit_length()):
        moved = step_bricks(moved, whole_bricks, power)
    previous = shifted_2(moved, "ybrick", 1)
    stacked = jnp.concatenate([previous, moved], axis=1).astype(jnp.float32)
    deskewed = jax.vmap(deskew_brick, in_axes=(0, 0, 0, None))(stacked, rests, fractions, brick)
    observed = deskewed.astype(jnp.float32) + BACKGROUND
    kernel_y = psf_y / jnp.sum(psf_y)
    kernel_x = psf_x / jnp.sum(psf_x)
    x_forward = band_matrix(kernel_x, 384, 128, RADIUS - 128)
    x_back = band_matrix(kernel_x[::-1], 384, 128, RADIUS - 128)
    y_back = band_matrix(kernel_y[::-1], brick + 2 * RADIUS, brick, 0)
    estimate = observed
    y_forward = band_matrix(kernel_y, brick + 2 * RADIUS, brick, 0)
    for turn_index in range(ITERS):
        extended = with_halo(estimate.astype(jnp.bfloat16), (("ybrick", 1),), RADIUS).astype(
            estimate.dtype
        )
        blurred = along_columns(along_rows(extended, y_forward), x_forward)
        ratio = observed / blurred
        ratio_wide = with_halo(ratio.astype(jnp.bfloat16), (("ybrick", 1),), RADIUS).astype(
            ratio.dtype
        )
        estimate = estimate * along_rows(along_columns(ratio_wide, x_back), y_back)
    return estimate


def column_windows(width):
    found = []
    for start in range(0, width, COLS):
        low, high = max(start - MARGIN, 0), min(start + COLS + MARGIN, width)
        found.append((start, low, high, low - (start - MARGIN)))
    return found


def plane_kernel(bricks, scalars, *refs):
    pieces, refs = refs[:bricks], refs[bricks:]
    left, right, x_forward, x_back, y_forward, y_back = refs[:6]
    outs, refs = refs[6 : 6 + bricks], refs[6 + bricks :]
    raw, observed, estimate, blur_in, back_in = refs
    brick_index, scan_index, last_scan, first_out = (scalars[i] for i in range(4))
    plane = pl.program_id(0)
    shift, fraction = scalars[4 + 2 * plane], scalars[5 + 2 * plane]
    _, brick, own = pieces[0].shape
    rows, width = observed.shape
    lead = raw.shape[0] - rows
    windows = column_windows(width)
    tiles = [(y, min(ROWS, rows - y)) for y in range(0, rows, ROWS)]

    raw[:lead, :] = jnp.zeros((lead, width), raw.dtype)
    for k in range(bricks):
        start = lead + (brick_index ^ k) * brick
        here = pl.ds(pl.multiple_of(start, ALIGN), brick)
        raw[here, :HALO] = left[0, k]
        raw[here, HALO : HALO + own] = pieces[k][0]
        raw[here, HALO + own :] = right[0, k]
    edge = jnp.zeros((RADIUS, width), blur_in.dtype)
    for buffer in (blur_in, back_in):
        buffer[:RADIUS, :] = edge
        buffer[RADIUS + rows :, :] = edge

    column = lax.broadcasted_iota(jnp.int32, (1, width), 1)
    inside = jnp.logical_and(
        jnp.logical_or(column >= HALO, scan_index > 0),
        jnp.logical_or(column < HALO + own, scan_index < last_scan),
    )
    weight = fraction.astype(jnp.float32) / NFRAC
    first = lead - shift - 1
    base = (first // ALIGN) * ALIGN
    depth = ROWS + ALIGN
    ahead = lax.broadcasted_iota(jnp.int32, (ROWS, depth), 1) - (
        lax.broadcasted_iota(jnp.int32, (ROWS, depth), 0) + (first - base)
    )
    mixing = jnp.where(ahead == 0, weight, jnp.where(ahead == 1, 1.0 - weight, 0.0))
    mixing = mixing.astype(jnp.bfloat16)
    for y, count in tiles:
        window = raw[pl.ds(pl.multiple_of(base + y, ALIGN), count + ALIGN), :]
        moved = jnp.dot(
            mixing[:count, : count + ALIGN], window, preferred_element_type=jnp.float32
        )
        level = moved.astype(jnp.bfloat16).astype(jnp.float32) + BACKGROUND
        level = jnp.where(inside, level, 0.0)
        observed[y : y + count, :] = level
        blur_in[RADIUS + y : RADIUS + y + count, :] = level.astype(jnp.bfloat16)

    for turn in range(ITERS):
        for y, count in tiles:
            wide = jnp.dot(
                y_forward[:count, : count + 2 * RADIUS],
                blur_in[y : y + count + 2 * RADIUS, :],
                preferred_element_type=jnp.float32,
            ).astype(jnp.bfloat16)
            ratios = []
            for start, low, high, row in windows:
                blurred = jnp.dot(
                    wide[:, low:high],
                    x_forward[row : row + high - low, :],
                    preferred_element_type=jnp.float32,
                )
                top = observed[y : y + count, start : start + COLS]
                ratios.append((top / jnp.maximum(blurred, TINY)).astype(jnp.bfloat16))
            ratio = jnp.concatenate(ratios, axis=1)
            for start, low, high, row in windows:
                back_in[RADIUS + y : RADIUS + y + count, start : start + COLS] = jnp.dot(
                    ratio[:, low:high],
                    x_back[row : row + high - low, :],
                    preferred_element_type=jnp.float32,
                ).astype(jnp.bfloat16)
        for y, count in tiles:
            correction = jnp.dot(
                y_back[:count, : count + 2 * RADIUS],
                back_in[y : y + count + 2 * RADIUS, :],
                preferred_element_type=jnp.float32,
            )
            before = observed if turn == 0 else estimate
            updated = before[y : y + count, :] * correction
            estimate[y : y + count, :] = updated
            if turn < ITERS - 1:
                blur_in[RADIUS + y : RADIUS + y + count, :] = updated.astype(jnp.bfloat16)
    for k in range(bricks):
        start = (first_out ^ k) * brick
        here = pl.ds(pl.multiple_of(start, ALIGN), brick)
        squared = jnp.square(estimate[here, HALO : HALO + own])
        outs[k][0] = jnp.square(squared).astype(outs[k].dtype)


def band_kernel(taps, x_forward, x_back, y_forward, y_back):
    row_sets = ((2, y_forward, 0, 0), (3, y_back, 0, 0), (1, x_forward, 1, 2), (0, x_back, 1, 2))
    for row, out, lead_blocks, spare_blocks in row_sets:
        count, width = out.shape
        line = taps[row : row + 1, :]
        line = line / jnp.sum(line)
        whole = width * (1 + lead_blocks + spare_blocks)
        line = jnp.concatenate(
            [line, jnp.zeros((1, whole - line.shape[1]), jnp.float32)], axis=1
        )
        begin = lead_blocks * width - lead_blocks * (MARGIN + RADIUS)
        band = pltpu.roll(
            jnp.broadcast_to(line, (count, whole)), begin, 1, stride=1, stride_axis=0
        )
        out[...] = band[:, lead_blocks * width : (1 + lead_blocks) * width].astype(out.dtype)


def band_matrices(psf_y, psf_x):
    rows = jnp.stack([psf_x, psf_x[::-1], psf_y, psf_y[::-1]])
    rows = jnp.pad(rows, ((0, 0), (0, 128 - rows.shape[1])))
    vmem = pl.BlockSpec(memory_space=pltpu.VMEM)
    shapes = [(COLS + 2 * MARGIN, COLS)] * 2 + [(ROWS, ROWS + 2 * RADIUS)] * 2
    return pl.pallas_call(
        band_kernel,
        out_shape=[jax.ShapeDtypeStruct(shape, jnp.bfloat16) for shape in shapes],
        in_specs=[vmem],
        out_specs=[vmem] * 4,
        compiler_params=pltpu.CompilerParams(vmem_limit_bytes=VMEM_BYTES),
        name="band_matrices",
    )(rows)


def deconvolve_planes(scalars, pieces, left, right, matrices, lead):
    bricks = len(pieces)
    count, brick, own = pieces[0].shape
    rows, width = bricks * brick, own + 2 * HALO
    vmem = pl.BlockSpec(memory_space=pltpu.VMEM)
    piece = pl.BlockSpec((1, brick, own), lambda j: (j, 0, 0))
    side = pl.BlockSpec((1, bricks, brick, HALO), lambda j: (j, 0, 0, 0))
    return pl.pallas_call(
        functools.partial(plane_kernel, bricks),
        grid=(count,),
        out_shape=[jax.ShapeDtypeStruct((count, brick, own), jnp.bfloat16)] * bricks,
        in_specs=[pl.BlockSpec(memory_space=pltpu.SMEM)]
        + [piece] * bricks
        + [side] * 2
        + [vmem] * 4,
        out_specs=[piece] * bricks,
        scratch_shapes=[
            pltpu.VMEM((lead + rows, width), jnp.bfloat16),
            pltpu.VMEM((rows, width), jnp.float32),
            pltpu.VMEM((rows, width), jnp.float32),
            pltpu.VMEM((rows + 2 * RADIUS, width), jnp.bfloat16),
            pltpu.VMEM((rows + 2 * RADIUS, width), jnp.bfloat16),
        ],
        compiler_params=pltpu.CompilerParams(vmem_limit_bytes=VMEM_BYTES),
        name="deconvolve_planes",
    )(scalars, *pieces, left, right, *matrices)


def edges_kernel(*refs):
    sources, outs = refs[:-2], refs[-2:]
    bricks = len(sources) // 2
    for side, out in enumerate(outs):
        for k in range(bricks):
            out[:, k] = sources[side * bricks + k][...]


def edges(pieces):
    bricks = len(pieces)
    count, brick, own = pieces[0].shape
    last = pl.BlockSpec((count, brick, HALO), lambda i: (0, 0, own // HALO - 1))
    first = pl.BlockSpec((count, brick, HALO), lambda i: (0, 0, 0))
    whole = pl.BlockSpec((count, bricks, brick, HALO), lambda i: (0, 0, 0, 0))
    return pl.pallas_call(
        edges_kernel,
        grid=(1,),
        out_shape=[jax.ShapeDtypeStruct((count, bricks, brick, HALO), jnp.bfloat16)] * 2,
        in_specs=[last] * bricks + [first] * bricks,
        out_specs=[whole] * 2,
        compiler_params=pltpu.CompilerParams(vmem_limit_bytes=VMEM_BYTES),
        name="edges",
    )(*pieces, *pieces)


def place_kernel(per_group, scans, bricks, position, *refs):
    pieces, out = refs[:-1], refs[-1]
    own = pieces[0].shape[2]
    count = pieces[0].shape[0]
    member, j = pl.program_id(0) // count, lax.rem(pl.program_id(0), count)
    for k in range(bricks):
        scan, its_member = source_of(position[0] ^ k, scans, per_group)

        @pl.when(its_member == member)
        def _(k=k, scan=scan):
            start = pl.multiple_of(scan * own, 128)
            piece = pieces[k][pl.ds(j, 1)].astype(out.dtype)
            out[:, :, pl.ds(start, own)] = jnp.sqrt(jnp.sqrt(piece))


def place_of(scan, brick, scans, per_group):
    half = scans // 2
    return ((scan % 2) * half + scan // 2) * per_group + brick % per_group


def source_of(place, scans, per_group):
    half = scans // 2
    scan = place // per_group
    return (scan % half) * 2 + scan // half, place % per_group


def by_planes(raw, row_shift, frac_index, psf_y, psf_x):
    planes, brick, own = raw.shape
    bricks, scans = lax.axis_size("ybrick"), lax.axis_size("scan")
    b, s = lax.axis_index("ybrick"), lax.axis_index("scan")
    own_planes = planes // bricks
    per_group = planes // scans // own_planes
    lead = bricks * brick // 4
    matrices = band_matrices(psf_y, psf_x)

    pieces = []
    for k in range(bricks):
        piece = lax.dynamic_slice_in_dim(raw, own_planes * (b ^ k), own_planes, 0)
        if k:
            piece = lax.ppermute(piece, "ybrick", [(i, i ^ k) for i in range(bricks)])
        pieces.append(piece)
    rightward = [(i, i + 1) for i in range(scans - 1)]
    lasts, firsts = edges(pieces)
    from_left = lax.ppermute(lasts, "scan", rightward)
    from_right = lax.ppermute(firsts, "scan", [(j, i) for i, j in rightward])

    position = place_of(s, b, scans, per_group)
    mine = [jnp.stack([b, s, scans - 1, position])]
    for table in (row_shift, frac_index):
        mine.append(lax.dynamic_slice_in_dim(table, own_planes * b, own_planes))
    scalars = jnp.concatenate([mine[0], jnp.stack(mine[1:], axis=1).reshape(-1)])
    done = deconvolve_planes(
        scalars.astype(jnp.int32), pieces, from_left, from_right, matrices, lead
    )
    arrived = []
    for k in range(bricks):
        pairs = []
        for i in range(scans):
            for m in range(bricks):
                place = place_of(i, m, scans, per_group) ^ k
                pairs.append((i * bricks + m, (m // per_group) * bricks + place))
        arrived.append(lax.ppermute(done[k], ("scan", "ybrick"), pairs))
    vmem = pl.BlockSpec(memory_space=pltpu.VMEM)
    return pl.pallas_call(
        functools.partial(place_kernel, per_group, scans, bricks),
        grid=(planes // scans,),
        out_shape=jax.ShapeDtypeStruct((planes // scans, brick, own * scans), jnp.float32),
        in_specs=[pl.BlockSpec(memory_space=pltpu.SMEM)] + [vmem] * len(arrived),
        out_specs=pl.BlockSpec((1, brick, own * scans), lambda i: (i, 0, 0)),
        compiler_params=pltpu.CompilerParams(vmem_limit_bytes=VMEM_BYTES),
        name="place_planes",
    )(b.astype(jnp.int32)[None], *arrived)


def local(raw, row_shift, frac_index, psf_y, psf_x):
    planes, brick, own = raw.shape
    bricks, scans = lax.axis_size("ybrick"), lax.axis_size("scan")
    fits = bricks & (bricks - 1) == 0 and scans % 2 == 0 and planes % bricks == 0
    fits = fits and (planes // scans) % (planes // bricks) == 0
    fits = fits and brick % ALIGN == 0 and own >= HALO and (own + 2 * HALO) % COLS == 0
    plan = by_planes if fits else by_bricks
    return plan(raw, row_shift, frac_index, psf_y, psf_x)


def solution(mesh):
    return jax.shard_map(
        local,
        mesh=mesh,
        in_specs=(P(None, "ybrick", "scan"), P(), P(), P(), P()),
        out_specs=P("scan", "ybrick", None),
        check_vma=False,
    )
```

profile of v0, /device:TPU:9, one launch (start us, length us, event | category | flops | bytes accessed | tf_op | source)
XLA Modules:
  0.0 137.7 jit_solution(6709824826051289430)
XLA Ops:
  0.0 1.6 %constant_dynamic-slice_fusion = (bf16[2,128,512]{2,1,0:T(8,128)(2,1)S(1)}, bf16[2,128,512]{2,1,0:T(8,128)(2,1)S(1)}, bf16[2,128,512]{2,1,0:T(8,128)(2,1)S(1)}, ...) fusion(bf16[16,128,512]{2,1,0:T(8,128)(2,1)} %param.5, ...), kind=kLoop, calls=%fused_computation.4 | loop fusion | bytes 4194336 | tf_op jit(solution)/shard_map/dynamic_slice | solution.py:338
  1.6 2.3 %collective-permute-start.6 = (bf16[2,128,512]{2,1,0:T(8,128)(2,1)S(1)}, bf16[2,128,512]{2,1,0:T(8,128)(2,1)S(1)}, u32[]{:S(2)}, u32[]{:S(2)}) collective-permute-start(bf16[2,128,512]{2,1,0:T(8,128)(2,1)S(1)} %get-tuple-element.33), channel_id=1, source_target_pairs={{0,7},{1,6},{2,5},{3,4},{4,3},{5,2},{6,1},{7,0},{8,15},{9,14},{10,... | collective-permute-start | bytes 786440 | tf_op jit(solution)/shard_map/ppermute | solution.py:340
  3.9 1.1 collective-permute-start.4
  5.0 1.2 collective-permute-start.3
  6.3 3.1 %collective-permute-start.2 = (bf16[2,128,512]{2,1,0:T(8,128)(2,1)S(1)}, bf16[2,128,512]{2,1,0:T(8,128)(2,1)S(1)}, u32[]{:S(2)}, u32[]{:S(2)}) collective-permute-start(bf16[2,128,512]{2,1,0:T(8,128)(2,1)S(1)} %get-tuple-element.36), channel_id=1, source_target_pairs={{0,3},{1,2},{2,1},{3,0},{4,7},{5,6},{6,5},{7,4},{8,11},{9,10},{10,... | collective-permute-start | bytes 786440 | tf_op jit(solution)/shard_map/ppermute | solution.py:340
  9.4 0.0 collective-permute-start.1
  9.4 19.5 %collective-permute-done.6.refs_7_.refs_15_ = bf16[2,128,512]{2,1,0:T(8,128)(2,1)S(1)} collective-permute-done((bf16[2,128,512]{2,1,0:T(8,128)(2,1)S(1)}, bf16[2,128,512]{2,1,0:T(8,128)(2,1)S(1)}, u32[]{:S(2)}, u32[]{:S(2)}) %collective-permute-start.6) | collective-permute-done | bytes 262176 | tf_op jit(solution)/shard_map/ppermute | solution.py:340
  28.9 1.2 collective-permute-start
  30.1 2.3 %collective-permute-done.4.refs_5_.refs_13_ = bf16[2,128,512]{2,1,0:T(8,128)(2,1)S(1)} collective-permute-done((bf16[2,128,512]{2,1,0:T(8,128)(2,1)S(1)}, bf16[2,128,512]{2,1,0:T(8,128)(2,1)S(1)}, u32[]{:S(2)}, u32[]{:S(2)}) %collective-permute-start.4) | collective-permute-done | bytes 262176 | tf_op jit(solution)/shard_map/ppermute | solution.py:340
  32.4 0.8 collective-permute-start.5
  33.2 10.3 %collective-permute-done.3.refs_4_.refs_12_ = bf16[2,128,512]{2,1,0:T(8,128)(2,1)S(1)} collective-permute-done((bf16[2,128,512]{2,1,0:T(8,128)(2,1)S(1)}, bf16[2,128,512]{2,1,0:T(8,128)(2,1)S(1)}, u32[]{:S(2)}, u32[]{:S(2)}) %collective-permute-start.3) | collective-permute-done | bytes 262176 | tf_op jit(solution)/shard_map/ppermute | solution.py:340
  43.5 0.0 collective-permute-done.2.refs_3_.refs_11_
  43.5 0.0 collective-permute-done.1.refs_2_.refs_10_
  43.5 0.0 collective-permute-done.refs_1_.refs_9_
  43.5 7.3 %collective-permute-done.5.refs_6_.refs_14_ = bf16[2,128,512]{2,1,0:T(8,128)(2,1)S(1)} collective-permute-done((bf16[2,128,512]{2,1,0:T(8,128)(2,1)S(1)}, bf16[2,128,512]{2,1,0:T(8,128)(2,1)S(1)}, u32[]{:S(2)}, u32[]{:S(2)}) %collective-permute-start.5) | collective-permute-done | bytes 262176 | tf_op jit(solution)/shard_map/ppermute | solution.py:340
  50.8 0.0 copy-start.6
  50.8 0.0 copy-start.7
  50.8 0.0 copy-start.4
  50.8 0.0 copy-start.5
  50.8 1.2 edges.1
  52.0 4.3 %collective-permute-start.7 = (bf16[2,8,128,128]{3,2,1,0:T(8,128)(2,1)}, bf16[2,8,128,128]{3,2,1,0:T(8,128)(2,1)S(1)}, u32[]{:S(2)}, u32[]{:S(2)}) collective-permute-start(bf16[2,8,128,128]{3,2,1,0:T(8,128)(2,1)} %get-tuple-element.19), channel_id=1, source_target_pairs={{0,8},{8,16},{16,24},{1,9},{9,17},{17,25},{2,10},{10,18},{18,26},{... | collective-permute-start | bytes 1572872 | tf_op jit(solution)/shard_map/ppermute | solution.py:344
  56.3 1.9 %collective-permute-start.8 = (bf16[2,8,128,128]{3,2,1,0:T(8,128)(2,1)}, bf16[2,8,128,128]{3,2,1,0:T(8,128)(2,1)S(1)}, u32[]{:S(2)}, u32[]{:S(2)}) collective-permute-start(bf16[2,8,128,128]{3,2,1,0:T(8,128)(2,1)} %get-tuple-element.20), channel_id=1, source_target_pairs={{8,0},{16,8},{24,16},{9,1},{17,9},{25,17},{10,2},{18,10},{26,18},{... | collective-permute-start | bytes 1572872 | tf_op jit(solution)/shard_map/ppermute | solution.py:345
  58.3 0.0 copy-done.6
  58.3 0.1 rev.7
  58.4 0.0 copy-done.7
  58.4 0.1 rev.6
  58.5 0.0 copy-done.4
  58.5 0.0 copy-done.5
  58.5 0.1 dynamic-slice_bitcast_fusion
  58.6 0.1 copy.6
  58.7 0.1 reshape.3
  58.8 0.2 band_matrices.1
  59.0 0.0 copy-start
  59.1 0.7 copy-done
  59.8 0.0 copy-start.2
  59.8 0.6 copy-done.2
  60.4 0.1 concatenate.3.scalars
  60.5 2.3 %collective-permute-done.7.refs_8_ = bf16[2,8,128,128]{3,2,1,0:T(8,128)(2,1)S(1)} collective-permute-done((bf16[2,8,128,128]{3,2,1,0:T(8,128)(2,1)}, bf16[2,8,128,128]{3,2,1,0:T(8,128)(2,1)S(1)}, u32[]{:S(2)}, u32[]{:S(2)}) %collective-permute-start.7) | collective-permute-done | bytes 524320 | tf_op jit(solution)/shard_map/ppermute | solution.py:344
  62.8 4.3 %collective-permute-done.8.refs_9_ = bf16[2,8,128,128]{3,2,1,0:T(8,128)(2,1)S(1)} collective-permute-done((bf16[2,8,128,128]{3,2,1,0:T(8,128)(2,1)}, bf16[2,8,128,128]{3,2,1,0:T(8,128)(2,1)S(1)}, u32[]{:S(2)}, u32[]{:S(2)}) %collective-permute-start.8) | collective-permute-done | bytes 524320 | tf_op jit(solution)/shard_map/ppermute | solution.py:345
  67.1 0.0 copy-start.1
  67.1 0.9 copy-done.1
  68.0 0.0 copy-start.3
  68.0 0.9 copy-done.3
  68.9 15.2 %deconvolve_planes.1 = (bf16[2,128,512]{2,1,0:T(8,128)(2,1)S(1)}, bf16[2,128,512]{2,1,0:T(8,128)(2,1)S(1)}, bf16[2,128,512]{2,1,0:T(8,128)(2,1)S(1)}, bf16[2,128...) custom-call(s32[8]{0:T(128)S(1)} %concatenate.3.scalars, ...), custom_call_target="tpu_custom_call" | custom-call | tf_op jit(solution)/shard_map/deconvolve_planes/pallas_call | solution.py:255
  84.1 2.8 %collective-permute-start.9 = (bf16[2,128,512]{2,1,0:T(8,128)(2,1)S(1)}, bf16[2,128,512]{2,1,0:T(8,128)(2,1)S(1)}, u32[]{:S(2)}, u32[]{:S(2)}) collective-permute-start(bf16[2,128,512]{2,1,0:T(8,128)(2,1)S(1)} %get-tuple-element.25), channel_id=1, source_target_pairs={{0,0},{1,1},{2,8},{3,9},{4,16},{5,17},{6,24},{7,25},{8,4},{9,5},{1... | collective-permute-start | bytes 786440 | tf_op jit(solution)/shard_map/ppermute | solution.py:362
  86.9 0.1 collective-permute-start.10
  87.0 0.1 collective-permute-start.11
  87.1 0.1 collective-permute-start.12
  87.1 2.0 %collective-permute-start.13 = (bf16[2,128,512]{2,1,0:T(8,128)(2,1)S(1)}, bf16[2,128,512]{2,1,0:T(8,128)(2,1)S(1)}, u32[]{:S(2)}, u32[]{:S(2)}) collective-permute-start(bf16[2,128,512]{2,1,0:T(8,128)(2,1)S(1)} %get-tuple-element.29), channel_id=1, source_target_pairs={{0,4},{1,5},{2,12},{3,13},{4,20},{5,21},{6,28},{7,29},{8,0},{9,1},... | collective-permute-start | bytes 786440 | tf_op jit(solution)/shard_map/ppermute | solution.py:362
  89.1 10.6 %collective-permute-done.9.refs_0_ = bf16[2,128,512]{2,1,0:T(8,128)(2,1)S(1)} collective-permute-done((bf16[2,128,512]{2,1,0:T(8,128)(2,1)S(1)}, bf16[2,128,512]{2,1,0:T(8,128)(2,1)S(1)}, u32[]{:S(2)}, u32[]{:S(2)}) %collective-permute-start.9) | collective-permute-done | bytes 262176 | tf_op jit(solution)/shard_map/ppermute | solution.py:362
  99.7 0.0 collective-permute-start.14
  99.7 17.6 %collective-permute-done.10.refs_1_ = bf16[2,128,512]{2,1,0:T(8,128)(2,1)S(1)} collective-permute-done((bf16[2,128,512]{2,1,0:T(8,128)(2,1)S(1)}, bf16[2,128,512]{2,1,0:T(8,128)(2,1)S(1)}, u32[]{:S(2)}, u32[]{:S(2)}) %collective-permute-start.10) | collective-permute-done | bytes 262176 | tf_op jit(solution)/shard_map/ppermute | solution.py:362
  117.3 0.7 collective-permute-start.15
  118.0 5.0 %collective-permute-done.11.refs_2_ = bf16[2,128,512]{2,1,0:T(8,128)(2,1)S(1)} collective-permute-done((bf16[2,128,512]{2,1,0:T(8,128)(2,1)S(1)}, bf16[2,128,512]{2,1,0:T(8,128)(2,1)S(1)}, u32[]{:S(2)}, u32[]{:S(2)}) %collective-permute-start.11) | collective-permute-done | bytes 262176 | tf_op jit(solution)/shard_map/ppermute | solution.py:362
  123.0 0.3 collective-permute-start.16
  123.2 3.5 %collective-permute-done.12.refs_3_ = bf16[2,128,512]{2,1,0:T(8,128)(2,1)S(1)} collective-permute-done((bf16[2,128,512]{2,1,0:T(8,128)(2,1)S(1)}, bf16[2,128,512]{2,1,0:T(8,128)(2,1)S(1)}, u32[]{:S(2)}, u32[]{:S(2)}) %collective-permute-start.12) | collective-permute-done | bytes 262176 | tf_op jit(solution)/shard_map/ppermute | solution.py:362
  126.8 0.0 collective-permute-done.13.refs_4_
  126.8 0.0 collective-permute-done.14.refs_5_
  126.8 0.0 collective-permute-done.15.refs_6_
  126.8 7.0 %collective-permute-done.16.refs_7_ = bf16[2,128,512]{2,1,0:T(8,128)(2,1)S(1)} collective-permute-done((bf16[2,128,512]{2,1,0:T(8,128)(2,1)S(1)}, bf16[2,128,512]{2,1,0:T(8,128)(2,1)S(1)}, u32[]{:S(2)}, u32[]{:S(2)}) %collective-permute-start.16) | collective-permute-done | bytes 262176 | tf_op jit(solution)/shard_map/ppermute | solution.py:362
  133.8 3.9 %place_planes.1 = f32[4,128,2048]{2,1,0:T(8,128)} custom-call(s32[1]{0:T(128)} %bitcast.position, bf16[2,128,512]{2,1,0:T(8,128)(2,1)S(1)} %collective-permute-done.9.refs_0_, bf16[2,128,512]{2,1,0:T(8,128)(2,1)S(1)} %collective-permute-done.10.refs_1_, bf16[2,128,512]{2,1,0:T(8,128)(2,1)S(1)} %collective-permute-done.11.refs_2_, ...), custom_call_target="tpu_custom_call" | custom-call | tf_op jit(solution)/shard_map/place_planes/pallas_call | solution.py:364
  (2 shorter events, 0.0 us)
Async XLA Ops:
  1.6 27.2 %collective-permute-start.6 = (bf16[2,128,512]{2,1,0:T(8,128)(2,1)S(1)}, bf16[2,128,512]{2,1,0:T(8,128)(2,1)S(1)}, u32[]{:S(2)}, u32[]{:S(2)}) collective-permute-start(bf16[2,128,512]{2,1,0:T(8,128)(2,1)S(1)} %get-tuple-element.33), channel_id=1, source_target_pairs={{0,7},{1,6},{2,5},{3,4},{4,3},{5,2},{6,1},{7,0},{8,15},{9,14},{10,... | collective-permute-start | bytes 786440 | tf_op jit(solution)/shard_map/ppermute | solution.py:340
  3.9 28.5 %collective-permute-start.4 = (bf16[2,128,512]{2,1,0:T(8,128)(2,1)S(1)}, bf16[2,128,512]{2,1,0:T(8,128)(2,1)S(1)}, u32[]{:S(2)}, u32[]{:S(2)}) collective-permute-start(bf16[2,128,512]{2,1,0:T(8,128)(2,1)S(1)} %get-tuple-element.34), channel_id=1, source_target_pairs={{0,5},{1,4},{2,7},{3,6},{4,1},{5,0},{6,3},{7,2},{8,13},{9,12},{10,... | collective-permute-start | bytes 786440 | tf_op jit(solution)/shard_map/ppermute | solution.py:340
  5.0 38.5 %collective-permute-start.3 = (bf16[2,128,512]{2,1,0:T(8,128)(2,1)S(1)}, bf16[2,128,512]{2,1,0:T(8,128)(2,1)S(1)}, u32[]{:S(2)}, u32[]{:S(2)}) collective-permute-start(bf16[2,128,512]{2,1,0:T(8,128)(2,1)S(1)} %get-tuple-element.35), channel_id=1, source_target_pairs={{0,4},{1,5},{2,6},{3,7},{4,0},{5,1},{6,2},{7,3},{8,12},{9,13},{10,... | collective-permute-start | bytes 786440 | tf_op jit(solution)/shard_map/ppermute | solution.py:340
  6.3 37.3 %collective-permute-start.2 = (bf16[2,128,512]{2,1,0:T(8,128)(2,1)S(1)}, bf16[2,128,512]{2,1,0:T(8,128)(2,1)S(1)}, u32[]{:S(2)}, u32[]{:S(2)}) collective-permute-start(bf16[2,128,512]{2,1,0:T(8,128)(2,1)S(1)} %get-tuple-element.36), channel_id=1, source_target_pairs={{0,3},{1,2},{2,1},{3,0},{4,7},{5,6},{6,5},{7,4},{8,11},{9,10},{10,... | collective-permute-start | bytes 786440 | tf_op jit(solution)/shard_map/ppermute | solution.py:340
  9.4 34.1 %collective-permute-start.1 = (bf16[2,128,512]{2,1,0:T(8,128)(2,1)S(1)}, bf16[2,128,512]{2,1,0:T(8,128)(2,1)S(1)}, u32[]{:S(2)}, u32[]{:S(2)}) collective-permute-start(bf16[2,128,512]{2,1,0:T(8,128)(2,1)S(1)} %get-tuple-element.37), channel_id=1, source_target_pairs={{0,2},{1,3},{2,0},{3,1},{4,6},{5,7},{6,4},{7,5},{8,10},{9,11},{10,... | collective-permute-start | bytes 786440 | tf_op jit(solution)/shard_map/ppermute | solution.py:340
  28.9 14.6 %collective-permute-start = (bf16[2,128,512]{2,1,0:T(8,128)(2,1)S(1)}, bf16[2,128,512]{2,1,0:T(8,128)(2,1)S(1)}, u32[]{:S(2)}, u32[]{:S(2)}) collective-permute-start(bf16[2,128,512]{2,1,0:T(8,128)(2,1)S(1)} %get-tuple-element.38), channel_id=1, source_target_pairs={{0,1},{1,0},{2,3},{3,2},{4,5},{5,4},{6,7},{7,6},{8,9},{9,8},{10,11... | collective-permute-start | bytes 786440 | tf_op jit(solution)/shard_map/ppermute | solution.py:340
  32.4 18.4 %collective-permute-start.5 = (bf16[2,128,512]{2,1,0:T(8,128)(2,1)S(1)}, bf16[2,128,512]{2,1,0:T(8,128)(2,1)S(1)}, u32[]{:S(2)}, u32[]{:S(2)}) collective-permute-start(bf16[2,128,512]{2,1,0:T(8,128)(2,1)S(1)} %get-tuple-element.40), channel_id=1, source_target_pairs={{0,6},{1,7},{2,4},{3,5},{4,2},{5,3},{6,0},{7,1},{8,14},{9,15},{10,... | collective-permute-start | bytes 786440 | tf_op jit(solution)/shard_map/ppermute | solution.py:340
  50.8 7.5 %copy-start.6 = (f32[65]{0:T(128)S(1)}, f32[65]{0:T(128)}, u32[]{:S(2)}) copy-start(f32[65]{0:T(128)} %param.8) | copy-start | bytes 784
  50.8 7.6 %copy-start.7 = (f32[65]{0:T(128)S(1)}, f32[65]{0:T(128)}, u32[]{:S(2)}) copy-start(f32[65]{0:T(128)} %param.9) | copy-start | bytes 784
  50.8 7.7 %copy-start.4 = (s32[16]{0:T(128)S(1)}, s32[16]{0:T(128)}, u32[]{:S(2)}) copy-start(s32[16]{0:T(128)} %param.7) | copy-start | bytes 196
  50.8 7.7 %copy-start.5 = (s32[16]{0:T(128)S(1)}, s32[16]{0:T(128)}, u32[]{:S(2)}) copy-start(s32[16]{0:T(128)} %param.6) | copy-start | bytes 196
  52.0 10.7 %collective-permute-start.7 = (bf16[2,8,128,128]{3,2,1,0:T(8,128)(2,1)}, bf16[2,8,128,128]{3,2,1,0:T(8,128)(2,1)S(1)}, u32[]{:S(2)}, u32[]{:S(2)}) collective-permute-start(bf16[2,8,128,128]{3,2,1,0:T(8,128)(2,1)} %get-tuple-element.19), channel_id=1, source_target_pairs={{0,8},{8,16},{16,24},{1,9},{9,17},{17,25},{2,10},{10,18},{18,26},{... | collective-permute-start | bytes 1572872 | tf_op jit(solution)/shard_map/ppermute | solution.py:344
  56.3 10.7 %collective-permute-start.8 = (bf16[2,8,128,128]{3,2,1,0:T(8,128)(2,1)}, bf16[2,8,128,128]{3,2,1,0:T(8,128)(2,1)S(1)}, u32[]{:S(2)}, u32[]{:S(2)}) collective-permute-start(bf16[2,8,128,128]{3,2,1,0:T(8,128)(2,1)} %get-tuple-element.20), channel_id=1, source_target_pairs={{8,0},{16,8},{24,16},{9,1},{17,9},{25,17},{10,2},{18,10},{26,18},{... | collective-permute-start | bytes 1572872 | tf_op jit(solution)/shard_map/ppermute | solution.py:345
  59.0 0.7 copy-start
  59.8 0.6 copy-start.2
  67.1 1.0 copy-start.1
  68.0 0.9 copy-start.3
  84.1 15.6 %collective-permute-start.9 = (bf16[2,128,512]{2,1,0:T(8,128)(2,1)S(1)}, bf16[2,128,512]{2,1,0:T(8,128)(2,1)S(1)}, u32[]{:S(2)}, u32[]{:S(2)}) collective-permute-start(bf16[2,128,512]{2,1,0:T(8,128)(2,1)S(1)} %get-tuple-element.25), channel_id=1, source_target_pairs={{0,0},{1,1},{2,8},{3,9},{4,16},{5,17},{6,24},{7,25},{8,4},{9,5},{1... | collective-permute-start | bytes 786440 | tf_op jit(solution)/shard_map/ppermute | solution.py:362
  86.9 30.4 %collective-permute-start.10 = (bf16[2,128,512]{2,1,0:T(8,128)(2,1)S(1)}, bf16[2,128,512]{2,1,0:T(8,128)(2,1)S(1)}, u32[]{:S(2)}, u32[]{:S(2)}) collective-permute-start(bf16[2,128,512]{2,1,0:T(8,128)(2,1)S(1)} %get-tuple-element.26), channel_id=1, source_target_pairs={{0,1},{1,0},{2,9},{3,8},{4,17},{5,16},{6,25},{7,24},{8,5},{9,4},{1... | collective-permute-start | bytes 786440 | tf_op jit(solution)/shard_map/ppermute | solution.py:362
  87.0 36.0 %collective-permute-start.11 = (bf16[2,128,512]{2,1,0:T(8,128)(2,1)S(1)}, bf16[2,128,512]{2,1,0:T(8,128)(2,1)S(1)}, u32[]{:S(2)}, u32[]{:S(2)}) collective-permute-start(bf16[2,128,512]{2,1,0:T(8,128)(2,1)S(1)} %get-tuple-element.27), channel_id=1, source_target_pairs={{0,2},{1,3},{2,10},{3,11},{4,18},{5,19},{6,26},{7,27},{8,6},{9,7},... | collective-permute-start | bytes 786440 | tf_op jit(solution)/shard_map/ppermute | solution.py:362
  87.1 39.7 %collective-permute-start.12 = (bf16[2,128,512]{2,1,0:T(8,128)(2,1)S(1)}, bf16[2,128,512]{2,1,0:T(8,128)(2,1)S(1)}, u32[]{:S(2)}, u32[]{:S(2)}) collective-permute-start(bf16[2,128,512]{2,1,0:T(8,128)(2,1)S(1)} %get-tuple-element.28), channel_id=1, source_target_pairs={{0,3},{1,2},{2,11},{3,10},{4,19},{5,18},{6,27},{7,26},{8,7},{9,6},... | collective-permute-start | bytes 786440 | tf_op jit(solution)/shard_map/ppermute | solution.py:362
  87.1 39.6 %collective-permute-start.13 = (bf16[2,128,512]{2,1,0:T(8,128)(2,1)S(1)}, bf16[2,128,512]{2,1,0:T(8,128)(2,1)S(1)}, u32[]{:S(2)}, u32[]{:S(2)}) collective-permute-start(bf16[2,128,512]{2,1,0:T(8,128)(2,1)S(1)} %get-tuple-element.29), channel_id=1, source_target_pairs={{0,4},{1,5},{2,12},{3,13},{4,20},{5,21},{6,28},{7,29},{8,0},{9,1},... | collective-permute-start | bytes 786440 | tf_op jit(solution)/shard_map/ppermute | solution.py:362
  99.7 27.1 %collective-permute-start.14 = (bf16[2,128,512]{2,1,0:T(8,128)(2,1)S(1)}, bf16[2,128,512]{2,1,0:T(8,128)(2,1)S(1)}, u32[]{:S(2)}, u32[]{:S(2)}) collective-permute-start(bf16[2,128,512]{2,1,0:T(8,128)(2,1)S(1)} %get-tuple-element.30), channel_id=1, source_target_pairs={{0,5},{1,4},{2,13},{3,12},{4,21},{5,20},{6,29},{7,28},{8,1},{9,0},... | collective-permute-start | bytes 786440 | tf_op jit(solution)/shard_map/ppermute | solution.py:362
  117.3 9.5 %collective-permute-start.15 = (bf16[2,128,512]{2,1,0:T(8,128)(2,1)S(1)}, bf16[2,128,512]{2,1,0:T(8,128)(2,1)S(1)}, u32[]{:S(2)}, u32[]{:S(2)}) collective-permute-start(bf16[2,128,512]{2,1,0:T(8,128)(2,1)S(1)} %get-tuple-element.31), channel_id=1, source_target_pairs={{0,6},{1,7},{2,14},{3,15},{4,22},{5,23},{6,30},{7,31},{8,2},{9,3},... | collective-permute-start | bytes 786440 | tf_op jit(solution)/shard_map/ppermute | solution.py:362
  123.0 10.8 %collective-permute-start.16 = (bf16[2,128,512]{2,1,0:T(8,128)(2,1)S(1)}, bf16[2,128,512]{2,1,0:T(8,128)(2,1)S(1)}, u32[]{:S(2)}, u32[]{:S(2)}) collective-permute-start(bf16[2,128,512]{2,1,0:T(8,128)(2,1)S(1)} %get-tuple-element.32), channel_id=1, source_target_pairs={{0,7},{1,6},{2,15},{3,14},{4,23},{5,22},{6,31},{7,30},{8,3},{9,2},... | collective-permute-start | bytes 786440 | tf_op jit(solution)/shard_map/ppermute | solution.py:362
where the time goes:
time: 140 us; the launch traced here: 138 us
  waiting for transfers between devices  89.7 us (64%)
  starting transfers between devices  22 us (16%)
  Pallas kernels  20.6 us (15%)
  local copies, waits for them, and re-layouts  5.36 us (4%)
    ppermute x8, waiting for transfers between devices, by_planes(): arrived.append(lax.ppermute(done[k], ('scan', 'ybrick'), pairs))  43.7 us
    ppermute x7, waiting for transfers between devices, by_planes(): piece = lax.ppermute(piece, 'ybrick', [(i, i ^ k) for i in range(bricks)])  39.4 us
    pallas_call x1, Pallas kernels, deconvolve_planes(): pl.pallas_call(functools.partial(plane_kernel, bricks), grid=(count,), ou...  15.2 us
    ppermute x7, starting transfers between devices, by_planes(): piece = lax.ppermute(piece, 'ybrick', [(i, i ^ k) for i in range(bricks)])  9.78 us
    ppermute x8, starting transfers between devices, by_planes(): arrived.append(lax.ppermute(done[k], ('scan', 'ybrick'), pairs))  5.94 us
    ppermute x1, starting transfers between devices, by_planes(): from_left = lax.ppermute(lasts, 'scan', rightward)  4.32 us
    ppermute x1, waiting for transfers between devices, by_planes(): from_right = lax.ppermute(firsts, 'scan', [(j, i) for i, j in rightward])  4.29 us
    pallas_call x1, Pallas kernels, by_planes(): pl.pallas_call(functools.partial(place_kernel, per_group, scans, bricks),...  3.93 us
  transfers between devices with their start and end apart: 17, of which 11 were waited for; matrix products, arithmetic and copies ran while one was open for 0% of the time, Pallas kernels for 0%

commit v1 on v0

--- a/solution.py
+++ b/solution.py
@@ -18,7 +18,8 @@
 MARGIN = 128
 ALIGN = 16
 TINY = 1e-30
-VMEM_BYTES = 32 * 2**20
+VMEM_BYTES = 24 * 2**20
+EARLY = 3
 
 
 def shifted_2(x, axis, by):
@@ -122,27 +123,38 @@
     return found
 
 
-def plane_kernel(bricks, scalars, *refs):
+def plane_kernel(bricks, j, scans, per_group, row_shift, frac_index, *refs):
     pieces, refs = refs[:bricks], refs[bricks:]
     left, right, x_forward, x_back, y_forward, y_back = refs[:6]
     outs, refs = refs[6 : 6 + bricks], refs[6 + bricks :]
-    raw, observed, estimate, blur_in, back_in = refs
-    brick_index, scan_index, last_scan, first_out = (scalars[i] for i in range(4))
-    plane = pl.program_id(0)
-    shift, fraction = scalars[4 + 2 * plane], scalars[5 + 2 * plane]
+    raw, observed, estimate, blur_in, back_in, arrived = refs
+    brick_index, scan_index = lax.axis_index("ybrick"), lax.axis_index("scan")
+    first_out = place_of(scan_index, brick_index, scans, per_group)
+    plane = row_shift.shape[0] // bricks * brick_index + j
+    shift, fraction = row_shift[plane], frac_index[plane]
     _, brick, own = pieces[0].shape
     rows, width = observed.shape
     lead = raw.shape[0] - rows
     windows = column_windows(width)
     tiles = [(y, min(ROWS, rows - y)) for y in range(0, rows, ROWS)]
 
+    copies = []
+    for k in range(bricks):
+        here = pl.ds(pl.multiple_of(lead + (brick_index ^ k) * brick, ALIGN), brick)
+        which = j if pieces[k].shape[0] > 1 else 0
+        for source, column, count in (
+            (pieces[k].at[which], HALO, own),
+            (left.at[0, k], 0, HALO),
+            (right.at[0, k], HALO + own, HALO),
+        ):
+            copies.append(
+                pltpu.make_async_copy(
+                    source, raw.at[here, pl.ds(column, count)], arrived.at[len(copies)]
+                )
+            )
+    for copy in copies:
+        copy.start()
     raw[:lead, :] = jnp.zeros((lead, width), raw.dtype)
-    for k in range(bricks):
-        start = lead + (brick_index ^ k) * brick
-        here = pl.ds(pl.multiple_of(start, ALIGN), brick)
-        raw[here, :HALO] = left[0, k]
-        raw[here, HALO : HALO + own] = pieces[k][0]
-        raw[here, HALO + own :] = right[0, k]
     edge = jnp.zeros((RADIUS, width), blur_in.dtype)
     for buffer in (blur_in, back_in):
         buffer[:RADIUS, :] = edge
@@ -151,7 +163,7 @@
     column = lax.broadcasted_iota(jnp.int32, (1, width), 1)
     inside = jnp.logical_and(
         jnp.logical_or(column >= HALO, scan_index > 0),
-        jnp.logical_or(column < HALO + own, scan_index < last_scan),
+        jnp.logical_or(column < HALO + own, scan_index < scans - 1),
     )
     weight = fraction.astype(jnp.float32) / NFRAC
     first = lead - shift - 1
@@ -162,6 +174,8 @@
     )
     mixing = jnp.where(ahead == 0, weight, jnp.where(ahead == 1, 1.0 - weight, 0.0))
     mixing = mixing.astype(jnp.bfloat16)
+    for copy in copies:
+        copy.wait()
     for y, count in tiles:
         window = raw[pl.ds(pl.multiple_of(base + y, ALIGN), count + ALIGN), :]
         moved = jnp.dot(
@@ -245,32 +259,39 @@
     )(rows)
 
 
-def deconvolve_planes(scalars, pieces, left, right, matrices, lead):
+def deconvolve_plane(j, scans, per_group, tables, pieces, left, right, matrices, lead):
     bricks = len(pieces)
-    count, brick, own = pieces[0].shape
+    _, brick, own = pieces[0].shape
     rows, width = bricks * brick, own + 2 * HALO
     vmem = pl.BlockSpec(memory_space=pltpu.VMEM)
-    piece = pl.BlockSpec((1, brick, own), lambda j: (j, 0, 0))
-    side = pl.BlockSpec((1, bricks, brick, HALO), lambda j: (j, 0, 0, 0))
+    smem = pl.BlockSpec(memory_space=pltpu.SMEM)
+    anywhere = pl.BlockSpec(memory_space=pl.ANY)
+    work = 2 * rows * width * (ITERS * 4 * COLS * 2)
     return pl.pallas_call(
-        functools.partial(plane_kernel, bricks),
-        grid=(count,),
-        out_shape=[jax.ShapeDtypeStruct((count, brick, own), jnp.bfloat16)] * bricks,
-        in_specs=[pl.BlockSpec(memory_space=pltpu.SMEM)]
-        + [piece] * bricks
-        + [side] * 2
-        + [vmem] * 4,
-        out_specs=[piece] * bricks,
+        functools.partial(plane_kernel, bricks, j, scans, per_group),
+        out_shape=[jax.ShapeDtypeStruct((1, brick, own), jnp.bfloat16)] * bricks,
+        in_specs=[smem] * 2 + [anywhere] * (bricks + 2) + [vmem] * 4,
+        out_specs=[vmem] * bricks,
         scratch_shapes=[
             pltpu.VMEM((lead + rows, width), jnp.bfloat16),
             pltpu.VMEM((rows, width), jnp.float32),
             pltpu.VMEM((rows, width), jnp.float32),
             pltpu.VMEM((rows + 2 * RADIUS, width), jnp.bfloat16),
             pltpu.VMEM((rows + 2 * RADIUS, width), jnp.bfloat16),
+            pltpu.SemaphoreType.DMA((3 * bricks,)),
         ],
+        cost_estimate=pl.CostEstimate(
+            flops=work, bytes_accessed=4 * rows * width, transcendentals=0
+        ),
         compiler_params=pltpu.CompilerParams(vmem_limit_bytes=VMEM_BYTES),
-        name="deconvolve_planes",
-    )(scalars, *pieces, left, right, *matrices)
+        name="deconvolve_plane",
+    )(*tables, *pieces, left, right, *matrices)
+
+
+def plane_block(piece, j, block=None, column=0):
+    count, brick, own = piece.shape
+    index = j if count > 1 else 0
+    return pl.BlockSpec((1, brick, block or own), lambda i: (index, 0, column))
 
 
 def edges_kernel(*refs):
@@ -281,36 +302,52 @@
             out[:, k] = sources[side * bricks + k][...]
 
 
-def edges(pieces):
+def edges(j, pieces):
     bricks = len(pieces)
-    count, brick, own = pieces[0].shape
-    last = pl.BlockSpec((count, brick, HALO), lambda i: (0, 0, own // HALO - 1))
-    first = pl.BlockSpec((count, brick, HALO), lambda i: (0, 0, 0))
-    whole = pl.BlockSpec((count, bricks, brick, HALO), lambda i: (0, 0, 0, 0))
+    _, brick, own = pieces[0].shape
+    last = [plane_block(p, j, HALO, own // HALO - 1) for p in pieces]
+    first = [plane_block(p, j, HALO, 0) for p in pieces]
+    whole = pl.BlockSpec((1, bricks, brick, HALO), lambda i: (0, 0, 0, 0))
     return pl.pallas_call(
         edges_kernel,
         grid=(1,),
-        out_shape=[jax.ShapeDtypeStruct((count, bricks, brick, HALO), jnp.bfloat16)] * 2,
-        in_specs=[last] * bricks + [first] * bricks,
+        out_shape=[jax.ShapeDtypeStruct((1, bricks, brick, HALO), jnp.bfloat16)] * 2,
+        in_specs=last + first,
         out_specs=[whole] * 2,
         compiler_params=pltpu.CompilerParams(vmem_limit_bytes=VMEM_BYTES),
         name="edges",
     )(*pieces, *pieces)
 
 
-def place_kernel(per_group, scans, bricks, position, *refs):
-    pieces, out = refs[:-1], refs[-1]
+def place_kernel(scans, per_group, bricks, *refs):
+    pieces, out = refs[:bricks], refs[-1]
     own = pieces[0].shape[2]
-    count = pieces[0].shape[0]
-    member, j = pl.program_id(0) // count, lax.rem(pl.program_id(0), count)
+    member = pl.program_id(0)
     for k in range(bricks):
-        scan, its_member = source_of(position[0] ^ k, scans, per_group)
+        scan, its_member = source_of(lax.axis_index("ybrick") ^ k, scans, per_group)
 
         @pl.when(its_member == member)
         def _(k=k, scan=scan):
             start = pl.multiple_of(scan * own, 128)
-            piece = pieces[k][pl.ds(j, 1)].astype(out.dtype)
+            piece = pieces[k][...].astype(out.dtype)
             out[:, :, pl.ds(start, own)] = jnp.sqrt(jnp.sqrt(piece))
+
+
+def place_plane(j, own_planes, per_group, scans, pieces, before):
+    bricks = len(pieces)
+    _, brick, own = pieces[0].shape
+    vmem = pl.BlockSpec(memory_space=pltpu.VMEM)
+    kept = [] if before is None else [before]
+    return pl.pallas_call(
+        functools.partial(place_kernel, scans, per_group, bricks),
+        grid=(per_group,),
+        out_shape=jax.ShapeDtypeStruct((per_group * own_planes, brick, own * scans), jnp.float32),
+        in_specs=[vmem] * bricks + [pl.BlockSpec(memory_space=pl.ANY)] * len(kept),
+        out_specs=pl.BlockSpec((1, brick, own * scans), lambda i: (i * own_planes + j, 0, 0)),
+        input_output_aliases={bricks: 0} if kept else {},
+        compiler_params=pltpu.CompilerParams(vmem_limit_bytes=VMEM_BYTES),
+        name="place_plane",
+    )(*pieces, *kept)
 
 
 def place_of(scan, brick, scans, per_group):
@@ -324,52 +361,67 @@
     return (scan % half) * 2 + scan // half, place % per_group
 
 
+def after(x, *earlier):
+    return lax.optimization_barrier((x, *earlier))[0]
+
+
 def by_planes(raw, row_shift, frac_index, psf_y, psf_x):
     planes, brick, own = raw.shape
     bricks, scans = lax.axis_size("ybrick"), lax.axis_size("scan")
-    b, s = lax.axis_index("ybrick"), lax.axis_index("scan")
+    b = lax.axis_index("ybrick")
     own_planes = planes // bricks
     per_group = planes // scans // own_planes
     lead = bricks * brick // 4
+    half = bricks // 2
     matrices = band_matrices(psf_y, psf_x)
 
-    pieces = []
-    for k in range(bricks):
-        piece = lax.dynamic_slice_in_dim(raw, own_planes * (b ^ k), own_planes, 0)
-        if k:
-            piece = lax.ppermute(piece, "ybrick", [(i, i ^ k) for i in range(bricks)])
-        pieces.append(piece)
+    def fetch(k, j, count, *earlier):
+        piece = lax.dynamic_slice_in_dim(raw, own_planes * (b ^ k) + j, count, 0)
+        if not k:
+            return piece
+        return lax.ppermute(
+            after(piece, *earlier), "ybrick", [(i, i ^ k) for i in range(bricks)]
+        )
+
     rightward = [(i, i + 1) for i in range(scans - 1)]
-    lasts, firsts = edges(pieces)
-    from_left = lax.ppermute(lasts, "scan", rightward)
-    from_right = lax.ppermute(firsts, "scan", [(j, i) for i, j in rightward])
-
-    position = place_of(s, b, scans, per_group)
-    mine = [jnp.stack([b, s, scans - 1, position])]
-    for table in (row_shift, frac_index):
-        mine.append(lax.dynamic_slice_in_dim(table, own_planes * b, own_planes))
-    scalars = jnp.concatenate([mine[0], jnp.stack(mine[1:], axis=1).reshape(-1)])
-    done = deconvolve_planes(
-        scalars.astype(jnp.int32), pieces, from_left, from_right, matrices, lead
-    )
-    arrived = []
-    for k in range(bricks):
-        pairs = []
-        for i in range(scans):
-            for m in range(bricks):
-                place = place_of(i, m, scans, per_group) ^ k
-                pairs.append((i * bricks + m, (m // per_group) * bricks + place))
-        arrived.append(lax.ppermute(done[k], ("scan", "ybrick"), pairs))
-    vmem = pl.BlockSpec(memory_space=pltpu.VMEM)
-    return pl.pallas_call(
-        functools.partial(place_kernel, per_group, scans, bricks),
-        grid=(planes // scans,),
-        out_shape=jax.ShapeDtypeStruct((planes // scans, brick, own * scans), jnp.float32),
-        in_specs=[pl.BlockSpec(memory_space=pltpu.SMEM)] + [vmem] * len(arrived),
-        out_specs=pl.BlockSpec((1, brick, own * scans), lambda i: (i, 0, 0)),
-        compiler_params=pltpu.CompilerParams(vmem_limit_bytes=VMEM_BYTES),
-        name="place_planes",
-    )(b.astype(jnp.int32)[None], *arrived)
+    leftward = [(j, i) for i, j in rightward]
+    far = [[] for _ in range(own_planes)]
+    near, sides, done = [], [], []
+    for j in range(own_planes):
+        for k in range(half, bricks):
+            earlier = ()
+            if j:
+                earlier = sides[j - 1] if k == bricks - 1 else (far[j - 1][k - half],)
+            far[j].append(fetch(k, j, 1, *earlier))
+        if not j:
+            near = [fetch(k, 0, own_planes) for k in range(half)]
+        pieces = near + far[j]
+        ends = pieces[:-1] + [after(pieces[-1], *(d[0] for d in done[-1:]))]
+        lasts, firsts = edges(j, ends)
+        sides.append(
+            (lax.ppermute(lasts, "scan", rightward), lax.ppermute(firsts, "scan", leftward))
+        )
+        done.append(
+            deconvolve_plane(
+                j, scans, per_group, (row_shift, frac_index), pieces, *sides[j], matrices, lead
+            )
+        )
+
+    out = None
+    for j in range(own_planes):
+        arrived = []
+        for k in range(bricks):
+            route = []
+            for i in range(scans):
+                for m in range(bricks):
+                    place = place_of(i, m, scans, per_group) ^ k
+                    route.append((i * bricks + m, (m // per_group) * bricks + place))
+            sent = done[j][k]
+            if j + 1 < own_planes and k >= EARLY:
+                sent = after(sent, *sides[j + 1])
+            arrived.append(lax.ppermute(sent, ("scan", "ybrick"), route))
+        out = place_plane(j, own_planes, per_group, scans, arrived, out)
+    return out
 
 
 def local(raw, row_shift, frac_index, psf_y, psf_x):

time: 140 us -> 128 us (0.914)
  the two profiles are of different devices: /device:TPU:9 before, /device:TPU:1 now
where the time goes in v1:
time: 128 us
  starting transfers between devices  67.9 us (53%)
  waiting for transfers between devices  35.5 us (28%)
  Pallas kernels  21.5 us (17%)
  local copies, waits for them, and re-layouts  2.68 us (2%)
    ppermute x16, starting transfers between devices, by_planes(): arrived.append(lax.ppermute(sent, ('scan', 'ybrick'), route))  30.9 us
    ppermute x11, starting transfers between devices, fetch(): lax.ppermute(after(piece, *earlier), 'ybrick', [(i, i ^ k) for i in range...  25.7 us
    ppermute x16, waiting for transfers between devices, by_planes(): arrived.append(lax.ppermute(sent, ('scan', 'ybrick'), route))  18.3 us
    ppermute x11, waiting for transfers between devices, fetch(): lax.ppermute(after(piece, *earlier), 'ybrick', [(i, i ^ k) for i in range...  17.2 us
    pallas_call x2, Pallas kernels, deconvolve_plane(): pl.pallas_call(functools.partial(plane_kernel, bricks, j, scans, per_grou...  16.5 us
    ppermute x2, starting transfers between devices, by_planes(): lax.ppermute(lasts, 'scan', rightward)  7.59 us
    pallas_call x2, Pallas kernels, place_plane(): pl.pallas_call(functools.partial(place_kernel, scans, per_group, bricks),...  4.5 us
    ppermute x2, starting transfers between devices, by_planes(): lax.ppermute(firsts, 'scan', leftward)  3.84 us
  transfers between devices with their start and end apart: 31, of which 9 were waited for; matrix products, arithmetic and copies ran while one was open for 0% of the time, Pallas kernels for 15%

profile of v1, /device:TPU:1, one launch (start us, length us, event | category | flops | bytes accessed | tf_op | source)
XLA Modules:
  0.0 127.9 jit_solution(14402883443977330972)
XLA Ops:
  0.0 2.3 %constant_dynamic-slice_fusion = (bf16[1,128,512]{2,1,0:T(8,128)(2,1)}, bf16[1,128,512]{2,1,0:T(8,128)(2,1)}, bf16[1,128,512]{2,1,0:T(8,128)(2,1)}, bf16[1,128,5...) fusion(bf16[16,128,512]{2,1,0:T(8,128)(2,1)} %param.5, ...), kind=kLoop, calls=%fused_computation | loop fusion | bytes 2097184 | tf_op jit(solution)/shard_map/dynamic_slice | solution.py:379
  2.3 4.2 %collective-permute-start.7 = (bf16[1,128,512]{2,1,0:T(8,128)(2,1)}, bf16[1,128,512]{2,1,0:T(8,128)(2,1)S(1)}, u32[]{:S(2)}, u32[]{:S(2)}) collective-permute-start(bf16[1,128,512]{2,1,0:T(8,128)(2,1)} %get-tuple-element.74), channel_id=1, source_target_pairs={{0,6},{1,7},{2,4},{3,5},{4,2},{5,3},{6,0},{7,1},{8,14},{9,15},{10,... | collective-permute-start | bytes 393224 | tf_op jit(solution)/shard_map/ppermute | solution.py:382
  6.5 1.0 collective-permute-start.9
  7.5 0.1 constant_dynamic-slice_fusion.8
  7.6 0.0 copy-start.8
  7.6 0.0 copy-start.9
  7.6 0.0 copy-start
  7.7 0.0 copy-start.1
  7.7 0.1 collective-permute-start.1
  7.7 1.4 %collective-permute-start.2 = (bf16[2,128,512]{2,1,0:T(8,128)(2,1)S(1)}, bf16[2,128,512]{2,1,0:T(8,128)(2,1)S(1)}, u32[]{:S(2)}, u32[]{:S(2)}) collective-permute-start(bf16[2,128,512]{2,1,0:T(8,128)(2,1)S(1)} %get-tuple-element.81), channel_id=1, source_target_pairs={{0,3},{1,2},{2,1},{3,0},{4,7},{5,6},{6,5},{7,4},{8,11},{9,10},{10,... | collective-permute-start | bytes 786440 | tf_op jit(solution)/shard_map/ppermute | solution.py:382
  9.2 1.2 collective-permute-start
  10.4 3.1 %collective-permute-start.5 = (bf16[1,128,512]{2,1,0:T(8,128)(2,1)S(1)}, bf16[1,128,512]{2,1,0:T(8,128)(2,1)S(1)}, u32[]{:S(2)}, u32[]{:S(2)}) collective-permute-start(bf16[1,128,512]{2,1,0:T(8,128)(2,1)S(1)} %copy-done.7), channel_id=1, source_target_pairs={{0,5},{1,4},{2,7},{3,6},{4,1},{5,0},{6,3},{7,2},{8,13},{9,12},{10,... | collective-permute-start | bytes 393224 | tf_op jit(solution)/shard_map/ppermute | solution.py:382
  13.5 5.9 %collective-permute-start.3 = (bf16[1,128,512]{2,1,0:T(8,128)(2,1)S(1)}, bf16[1,128,512]{2,1,0:T(8,128)(2,1)S(1)}, u32[]{:S(2)}, u32[]{:S(2)}) collective-permute-start(bf16[1,128,512]{2,1,0:T(8,128)(2,1)S(1)} %copy-done.6), channel_id=1, source_target_pairs={{0,4},{1,5},{2,6},{3,7},{4,0},{5,1},{6,2},{7,3},{8,12},{9,13},{10,... | collective-permute-start | bytes 393224 | tf_op jit(solution)/shard_map/ppermute | solution.py:382
  19.4 6.4 %collective-permute-done.5.refs_5_.refs_13_ = bf16[1,128,512]{2,1,0:T(8,128)(2,1)S(1)} collective-permute-done((bf16[1,128,512]{2,1,0:T(8,128)(2,1)S(1)}, bf16[1,128,512]{2,1,0:T(8,128)(2,1)S(1)}, u32[]{:S(2)}, u32[]{:S(2)}) %collective-permute-start.5) | collective-permute-done | bytes 131104 | tf_op jit(solution)/shard_map/ppermute | solution.py:382
  25.8 2.8 %collective-permute-done.3.refs_4_.refs_12_ = bf16[1,128,512]{2,1,0:T(8,128)(2,1)S(1)} collective-permute-done((bf16[1,128,512]{2,1,0:T(8,128)(2,1)S(1)}, bf16[1,128,512]{2,1,0:T(8,128)(2,1)S(1)}, u32[]{:S(2)}, u32[]{:S(2)}) %collective-permute-start.3) | collective-permute-done | bytes 131104 | tf_op jit(solution)/shard_map/ppermute | solution.py:382
  28.6 2.7 %collective-permute-done.2.refs_3_.refs_11_ = bf16[2,128,512]{2,1,0:T(8,128)(2,1)S(1)} collective-permute-done((bf16[2,128,512]{2,1,0:T(8,128)(2,1)S(1)}, bf16[2,128,512]{2,1,0:T(8,128)(2,1)S(1)}, u32[]{:S(2)}, u32[]{:S(2)}) %collective-permute-start.2) | collective-permute-done | bytes 262176 | tf_op jit(solution)/shard_map/ppermute | solution.py:382
  31.4 0.0 collective-permute-done.refs_1_.refs_9_
  31.4 0.1 edges.2
  31.5 3.5 %collective-permute-start.10 = (bf16[1,8,128,128]{3,2,1,0:T(8,128)(2,1)S(1)}, bf16[1,8,128,128]{3,2,1,0:T(8,128)(2,1)S(1)}, u32[]{:S(2)}, u32[]{:S(2)}) collective-permute-start(bf16[1,8,128,128]{3,2,1,0:T(8,128)(2,1)S(1)} %get-tuple-element.42), channel_id=1, source_target_pairs={{0,8},{8,16},{16,24},{1,9},{9,17},{17,25},{2,10},{10,18},{18,26},{... | collective-permute-start | bytes 786440 | tf_op jit(solution)/shard_map/ppermute | solution.py:402
  35.0 1.9 %collective-permute-start.11 = (bf16[1,8,128,128]{3,2,1,0:T(8,128)(2,1)S(1)}, bf16[1,8,128,128]{3,2,1,0:T(8,128)(2,1)S(1)}, u32[]{:S(2)}, u32[]{:S(2)}) collective-permute-start(bf16[1,8,128,128]{3,2,1,0:T(8,128)(2,1)S(1)} %get-tuple-element.43), channel_id=1, source_target_pairs={{8,0},{16,8},{24,16},{9,1},{17,9},{25,17},{10,2},{18,10},{26,18},{... | collective-permute-start | bytes 786440 | tf_op jit(solution)/shard_map/ppermute | solution.py:402
  37.0 0.1 rev.7
  37.1 0.1 rev.6
  37.2 0.2 band_matrices.1
  37.4 3.3 %collective-permute-start.8 = (bf16[1,128,512]{2,1,0:T(8,128)(2,1)S(1)}, bf16[1,128,512]{2,1,0:T(8,128)(2,1)S(1)}, u32[]{:S(2)}, u32[]{:S(2)}) collective-permute-start(bf16[1,128,512]{2,1,0:T(8,128)(2,1)S(1)} %copy-done.4), channel_id=1, source_target_pairs={{0,6},{1,7},{2,4},{3,5},{4,2},{5,3},{6,0},{7,1},{8,14},{9,15},{10,... | collective-permute-start | bytes 393224 | tf_op jit(solution)/shard_map/ppermute | solution.py:382
  40.8 2.3 %collective-permute-start.4 = (bf16[1,128,512]{2,1,0:T(8,128)(2,1)S(1)}, bf16[1,128,512]{2,1,0:T(8,128)(2,1)S(1)}, u32[]{:S(2)}, u32[]{:S(2)}) collective-permute-start(bf16[1,128,512]{2,1,0:T(8,128)(2,1)S(1)} %get-tuple-element.39), channel_id=1, source_target_pairs={{0,4},{1,5},{2,6},{3,7},{4,0},{5,1},{6,2},{7,3},{8,12},{9,13},{10,... | collective-permute-start | bytes 393224 | tf_op jit(solution)/shard_map/ppermute | solution.py:382
  43.1 0.0 collective-permute-done.10.refs_8_
  43.1 0.0 collective-permute-done.11.refs_9_
  43.1 3.1 %collective-permute-start.12 = (bf16[1,128,512]{2,1,0:T(8,128)(2,1)S(1)}, bf16[1,128,512]{2,1,0:T(8,128)(2,1)S(1)}, u32[]{:S(2)}, u32[]{:S(2)}) collective-permute-start(bf16[1,128,512]{2,1,0:T(8,128)(2,1)S(1)} %copy-done.5), channel_id=1, source_target_pairs={{0,7},{1,6},{2,5},{3,4},{4,3},{5,2},{6,1},{7,0},{8,15},{9,14},{10,... | collective-permute-start | bytes 393224 | tf_op jit(solution)/shard_map/ppermute | solution.py:382
  46.3 8.2 %deconvolve_plane.2 = (bf16[1,128,512]{2,1,0:T(8,128)(2,1)S(1)}, bf16[1,128,512]{2,1,0:T(8,128)(2,1)S(1)}, bf16[1,128,512]{2,1,0:T(8,128)(2,1)S(1)}, bf16[1,128,...) custom-call(s32[16]{0:T(128)S(1)} %copy-done, ...), custom_call_target="tpu_custom_call" | custom-call | flops 6442450944 | bytes 3145728 | tf_op jit(solution)/shard_map/deconvolve_plane/pallas_call | solution.py:270
  54.5 0.0 collective-permute-done.8.refs_6_.refs_14_
  54.5 2.4 %collective-permute-done.6.refs_5_.refs_13_ = bf16[1,128,512]{2,1,0:T(8,128)(2,1)S(1)} collective-permute-done((bf16[1,128,512]{2,1,0:T(8,128)(2,1)S(1)}, bf16[1,128,512]{2,1,0:T(8,128)(2,1)S(1)}, u32[]{:S(2)}, u32[]{:S(2)}) %collective-permute-start.6) | collective-permute-done | bytes 131104 | tf_op jit(solution)/shard_map/ppermute | solution.py:382
  56.9 2.9 %collective-permute-done.4.refs_4_.refs_12_ = bf16[1,128,512]{2,1,0:T(8,128)(2,1)S(1)} collective-permute-done((bf16[1,128,512]{2,1,0:T(8,128)(2,1)S(1)}, bf16[1,128,512]{2,1,0:T(8,128)(2,1)S(1)}, u32[]{:S(2)}, u32[]{:S(2)}) %collective-permute-start.4) | collective-permute-done | bytes 131104 | tf_op jit(solution)/shard_map/ppermute | solution.py:382
  59.8 0.1 edges.3
  59.9 4.1 %collective-permute-start.13 = (bf16[1,8,128,128]{3,2,1,0:T(8,128)(2,1)S(1)}, bf16[1,8,128,128]{3,2,1,0:T(8,128)(2,1)S(1)}, u32[]{:S(2)}, u32[]{:S(2)}) collective-permute-start(bf16[1,8,128,128]{3,2,1,0:T(8,128)(2,1)S(1)} %get-tuple-element.51), channel_id=1, source_target_pairs={{0,8},{8,16},{16,24},{1,9},{9,17},{17,25},{2,10},{10,18},{18,26},{... | collective-permute-start | bytes 786440 | tf_op jit(solution)/shard_map/ppermute | solution.py:402
  64.0 1.9 %collective-permute-start.14 = (bf16[1,8,128,128]{3,2,1,0:T(8,128)(2,1)S(1)}, bf16[1,8,128,128]{3,2,1,0:T(8,128)(2,1)S(1)}, u32[]{:S(2)}, u32[]{:S(2)}) collective-permute-start(bf16[1,8,128,128]{3,2,1,0:T(8,128)(2,1)S(1)} %get-tuple-element.52), channel_id=1, source_target_pairs={{8,0},{16,8},{24,16},{9,1},{17,9},{25,17},{10,2},{18,10},{26,18},{... | collective-permute-start | bytes 786440 | tf_op jit(solution)/shard_map/ppermute | solution.py:402
  65.9 1.2 collective-permute-start.24
  67.1 5.1 %collective-permute-start.23 = (bf16[1,128,512]{2,1,0:T(8,128)(2,1)S(1)}, bf16[1,128,512]{2,1,0:T(8,128)(2,1)S(1)}, u32[]{:S(2)}, u32[]{:S(2)}) collective-permute-start(bf16[1,128,512]{2,1,0:T(8,128)(2,1)S(1)} %get-tuple-element.49), channel_id=1, source_target_pairs={{0,0},{1,1},{2,8},{3,9},{4,16},{5,17},{6,24},{7,25},{8,4},{9,5},{1... | collective-permute-start | bytes 393224 | tf_op jit(solution)/shard_map/ppermute | solution.py:422
  72.2 0.4 collective-permute-start.25
  72.6 0.0 collective-permute-done.13.refs_8_
  72.6 0.0 collective-permute-done.14.refs_9_
  72.7 4.7 %collective-permute-start.26 = (bf16[1,128,512]{2,1,0:T(8,128)(2,1)S(1)}, bf16[1,128,512]{2,1,0:T(8,128)(2,1)S(1)}, u32[]{:S(2)}, u32[]{:S(2)}) collective-permute-start(bf16[1,128,512]{2,1,0:T(8,128)(2,1)S(1)} %get-tuple-element.64), channel_id=1, source_target_pairs={{0,3},{1,2},{2,11},{3,10},{4,19},{5,18},{6,27},{7,26},{8,7},{9,6},... | collective-permute-start | bytes 393224 | tf_op jit(solution)/shard_map/ppermute | solution.py:422
  77.3 0.0 collective-permute-start.27
  77.3 0.0 collective-permute-done.24.refs_1_
  77.3 2.9 %collective-permute-start.28 = (bf16[1,128,512]{2,1,0:T(8,128)(2,1)S(1)}, bf16[1,128,512]{2,1,0:T(8,128)(2,1)S(1)}, u32[]{:S(2)}, u32[]{:S(2)}) collective-permute-start(bf16[1,128,512]{2,1,0:T(8,128)(2,1)S(1)} %get-tuple-element.68), channel_id=1, source_target_pairs={{0,5},{1,4},{2,13},{3,12},{4,21},{5,20},{6,29},{7,28},{8,1},{9,0},... | collective-permute-start | bytes 393224 | tf_op jit(solution)/shard_map/ppermute | solution.py:422
  80.2 8.2 %deconvolve_plane.3 = (bf16[1,128,512]{2,1,0:T(8,128)(2,1)S(1)}, bf16[1,128,512]{2,1,0:T(8,128)(2,1)S(1)}, bf16[1,128,512]{2,1,0:T(8,128)(2,1)S(1)}, bf16[1,128,...) custom-call(s32[16]{0:T(128)S(1)} %copy-done, ...), custom_call_target="tpu_custom_call" | custom-call | flops 6442450944 | bytes 3145728 | tf_op jit(solution)/shard_map/deconvolve_plane/pallas_call | solution.py:270
  88.4 0.0 collective-permute-done.25.refs_2_
  88.4 1.9 %collective-permute-start.29 = (bf16[1,128,512]{2,1,0:T(8,128)(2,1)S(1)}, bf16[1,128,512]{2,1,0:T(8,128)(2,1)S(1)}, u32[]{:S(2)}, u32[]{:S(2)}) collective-permute-start(bf16[1,128,512]{2,1,0:T(8,128)(2,1)S(1)} %get-tuple-element.70), channel_id=1, source_target_pairs={{0,6},{1,7},{2,14},{3,15},{4,22},{5,23},{6,30},{7,31},{8,2},{9,3},... | collective-permute-start | bytes 393224 | tf_op jit(solution)/shard_map/ppermute | solution.py:422
  90.4 0.0 collective-permute-done.23.refs_0_
  90.4 4.5 %collective-permute-start.30 = (bf16[1,128,512]{2,1,0:T(8,128)(2,1)S(1)}, bf16[1,128,512]{2,1,0:T(8,128)(2,1)S(1)}, u32[]{:S(2)}, u32[]{:S(2)}) collective-permute-start(bf16[1,128,512]{2,1,0:T(8,128)(2,1)S(1)} %get-tuple-element.72), channel_id=1, source_target_pairs={{0,7},{1,6},{2,15},{3,14},{4,23},{5,22},{6,31},{7,30},{8,3},{9,2},... | collective-permute-start | bytes 393224 | tf_op jit(solution)/shard_map/ppermute | solution.py:422
  94.8 0.0 collective-permute-done.26.refs_3_
  94.9 1.9 %collective-permute-start.15 = (bf16[1,128,512]{2,1,0:T(8,128)(2,1)S(1)}, bf16[1,128,512]{2,1,0:T(8,128)(2,1)S(1)}, u32[]{:S(2)}, u32[]{:S(2)}) collective-permute-start(bf16[1,128,512]{2,1,0:T(8,128)(2,1)S(1)} %get-tuple-element.53), channel_id=1, source_target_pairs={{0,0},{1,1},{2,8},{3,9},{4,16},{5,17},{6,24},{7,25},{8,4},{9,5},{1... | collective-permute-start | bytes 393224 | tf_op jit(solution)/shard_map/ppermute | solution.py:422
  96.8 1.3 %collective-permute-start.16 = (bf16[1,128,512]{2,1,0:T(8,128)(2,1)S(1)}, bf16[1,128,512]{2,1,0:T(8,128)(2,1)S(1)}, u32[]{:S(2)}, u32[]{:S(2)}) collective-permute-start(bf16[1,128,512]{2,1,0:T(8,128)(2,1)S(1)} %get-tuple-element.54), channel_id=1, source_target_pairs={{0,1},{1,0},{2,9},{3,8},{4,17},{5,16},{6,25},{7,24},{8,5},{9,4},{1... | collective-permute-start | bytes 393224 | tf_op jit(solution)/shard_map/ppermute | solution.py:422
  98.1 3.3 %collective-permute-start.17 = (bf16[1,128,512]{2,1,0:T(8,128)(2,1)S(1)}, bf16[1,128,512]{2,1,0:T(8,128)(2,1)S(1)}, u32[]{:S(2)}, u32[]{:S(2)}) collective-permute-start(bf16[1,128,512]{2,1,0:T(8,128)(2,1)S(1)} %get-tuple-element.55), channel_id=1, source_target_pairs={{0,2},{1,3},{2,10},{3,11},{4,18},{5,19},{6,26},{7,27},{8,6},{9,7},... | collective-permute-start | bytes 393224 | tf_op jit(solution)/shard_map/ppermute | solution.py:422
  101.5 1.6 %collective-permute-start.18 = (bf16[1,128,512]{2,1,0:T(8,128)(2,1)S(1)}, bf16[1,128,512]{2,1,0:T(8,128)(2,1)S(1)}, u32[]{:S(2)}, u32[]{:S(2)}) collective-permute-start(bf16[1,128,512]{2,1,0:T(8,128)(2,1)S(1)} %get-tuple-element.56), channel_id=1, source_target_pairs={{0,3},{1,2},{2,11},{3,10},{4,19},{5,18},{6,27},{7,26},{8,7},{9,6},... | collective-permute-start | bytes 393224 | tf_op jit(solution)/shard_map/ppermute | solution.py:422
  103.1 0.0 collective-permute-done.30.refs_7_
  103.1 2.9 %collective-permute-done.15.refs_0_ = bf16[1,128,512]{2,1,0:T(8,128)(2,1)S(1)} collective-permute-done((bf16[1,128,512]{2,1,0:T(8,128)(2,1)S(1)}, bf16[1,128,512]{2,1,0:T(8,128)(2,1)S(1)}, u32[]{:S(2)}, u32[]{:S(2)}) %collective-permute-start.15) | collective-permute-done | bytes 131104 | tf_op jit(solution)/shard_map/ppermute | solution.py:422
  106.0 0.0 collective-permute-start.20
  106.0 8.4 %collective-permute-done.16.refs_1_ = bf16[1,128,512]{2,1,0:T(8,128)(2,1)S(1)} collective-permute-done((bf16[1,128,512]{2,1,0:T(8,128)(2,1)S(1)}, bf16[1,128,512]{2,1,0:T(8,128)(2,1)S(1)}, u32[]{:S(2)}, u32[]{:S(2)}) %collective-permute-start.16) | collective-permute-done | bytes 131104 | tf_op jit(solution)/shard_map/ppermute | solution.py:422
  114.4 1.9 %collective-permute-start.21 = (bf16[1,128,512]{2,1,0:T(8,128)(2,1)S(1)}, bf16[1,128,512]{2,1,0:T(8,128)(2,1)S(1)}, u32[]{:S(2)}, u32[]{:S(2)}) collective-permute-start(bf16[1,128,512]{2,1,0:T(8,128)(2,1)S(1)} %get-tuple-element.59), channel_id=1, source_target_pairs={{0,6},{1,7},{2,14},{3,15},{4,22},{5,23},{6,30},{7,31},{8,2},{9,3},... | collective-permute-start | bytes 393224 | tf_op jit(solution)/shard_map/ppermute | solution.py:422
  116.3 0.1 collective-permute-start.22
  116.4 2.3 %place_plane.2.refs_8_ = f32[4,128,2048]{2,1,0:T(8,128)} custom-call(bf16[1,128,512]{2,1,0:T(8,128)(2,1)S(1)} %collective-permute-done.23.refs_0_, bf16[1,128,512]{2,1,0:T(8,128)(2,1)S(1)} %collective-permute-done.24.refs_1_, bf16[1,128,512]{2,1,0:T(8,128)(2,1)S(1)} %collective-permute-done.25.refs_2_, ...), custom_call_target="tpu_custom_call" | custom-call | tf_op jit(solution)/shard_map/place_plane/pallas_call | solution.py:341
  118.7 5.5 %collective-permute-done.21.refs_6_ = bf16[1,128,512]{2,1,0:T(8,128)(2,1)S(1)} collective-permute-done((bf16[1,128,512]{2,1,0:T(8,128)(2,1)S(1)}, bf16[1,128,512]{2,1,0:T(8,128)(2,1)S(1)}, u32[]{:S(2)}, u32[]{:S(2)}) %collective-permute-start.21) | collective-permute-done | bytes 131104 | tf_op jit(solution)/shard_map/ppermute | solution.py:422
  124.2 1.4 %collective-permute-done.22.refs_7_ = bf16[1,128,512]{2,1,0:T(8,128)(2,1)S(1)} collective-permute-done((bf16[1,128,512]{2,1,0:T(8,128)(2,1)S(1)}, bf16[1,128,512]{2,1,0:T(8,128)(2,1)S(1)}, u32[]{:S(2)}, u32[]{:S(2)}) %collective-permute-start.22) | collective-permute-done | bytes 131104 | tf_op jit(solution)/shard_map/ppermute | solution.py:422
  125.6 2.2 %place_plane.3 = f32[4,128,2048]{2,1,0:T(8,128)} custom-call(bf16[1,128,512]{2,1,0:T(8,128)(2,1)S(1)} %collective-permute-done.15.refs_0_, bf16[1,128,512]{2,1,0:T(8,128)(2,1)S(1)} %collective-permute-done.16.refs_1_, bf16[1,128,512]{2,1,0:T(8,128)(2,1)S(1)} %collective-permute-done.17.refs_2_, ...), custom_call_target="tpu_custom_call", output_to_operand_aliasing={{}: (8, {})} | custom-call | tf_op jit(solution)/shard_map/place_plane/pallas_call | solution.py:341
  (30 shorter events, 0.1 us)
Async XLA Ops:
  0.0 7.5 %copy-start.2 = (bf16[16,128,512]{2,1,0:T(8,128)(2,1)S(1)}, bf16[16,128,512]{2,1,0:T(8,128)(2,1)}, u32[]{:S(2)}) copy-start(bf16[16,128,512]{2,1,0:T(8,128)(2,1)} %param.5) | copy-start | bytes 6291460
  2.3 8.0 %collective-permute-start.7 = (bf16[1,128,512]{2,1,0:T(8,128)(2,1)}, bf16[1,128,512]{2,1,0:T(8,128)(2,1)S(1)}, u32[]{:S(2)}, u32[]{:S(2)}) collective-permute-start(bf16[1,128,512]{2,1,0:T(8,128)(2,1)} %get-tuple-element.74), channel_id=1, source_target_pairs={{0,6},{1,7},{2,4},{3,5},{4,2},{5,3},{6,0},{7,1},{8,14},{9,15},{10,... | collective-permute-start | bytes 393224 | tf_op jit(solution)/shard_map/ppermute | solution.py:382
  6.5 7.0 %collective-permute-start.9 = (bf16[1,128,512]{2,1,0:T(8,128)(2,1)}, bf16[1,128,512]{2,1,0:T(8,128)(2,1)S(1)}, u32[]{:S(2)}, u32[]{:S(2)}) collective-permute-start(bf16[1,128,512]{2,1,0:T(8,128)(2,1)} %get-tuple-element.73), channel_id=1, source_target_pairs={{0,7},{1,6},{2,5},{3,4},{4,3},{5,2},{6,1},{7,0},{8,15},{9,14},{10,... | collective-permute-start | bytes 393224 | tf_op jit(solution)/shard_map/ppermute | solution.py:382
  7.5 2.9 %copy-start.7 = (bf16[1,128,512]{2,1,0:T(8,128)(2,1)S(1)}, bf16[1,128,512]{2,1,0:T(8,128)(2,1)}, u32[]{:S(2)}) copy-start(bf16[1,128,512]{2,1,0:T(8,128)(2,1)} %get-tuple-element.76) | copy-start | bytes 393220
  7.5 6.0 %copy-start.6 = (bf16[1,128,512]{2,1,0:T(8,128)(2,1)S(1)}, bf16[1,128,512]{2,1,0:T(8,128)(2,1)}, u32[]{:S(2)}) copy-start(bf16[1,128,512]{2,1,0:T(8,128)(2,1)} %get-tuple-element.78) | copy-start | bytes 393220
  7.6 29.4 %copy-start.8 = (f32[65]{0:T(128)S(1)}, f32[65]{0:T(128)}, u32[]{:S(2)}) copy-start(f32[65]{0:T(128)} %param.8) | copy-start | bytes 784
  7.6 29.5 %copy-start.9 = (f32[65]{0:T(128)S(1)}, f32[65]{0:T(128)}, u32[]{:S(2)}) copy-start(f32[65]{0:T(128)} %param.9) | copy-start | bytes 784
  7.6 29.8 %copy-start.4 = (bf16[1,128,512]{2,1,0:T(8,128)(2,1)S(1)}, bf16[1,128,512]{2,1,0:T(8,128)(2,1)}, u32[]{:S(2)}) copy-start(bf16[1,128,512]{2,1,0:T(8,128)(2,1)} %get-tuple-element.41) | copy-start | bytes 393220
  7.6 33.1 %copy-start.3 = (bf16[1,128,512]{2,1,0:T(8,128)(2,1)S(1)}, bf16[1,128,512]{2,1,0:T(8,128)(2,1)}, u32[]{:S(2)}) copy-start(bf16[1,128,512]{2,1,0:T(8,128)(2,1)} %get-tuple-element.40) | copy-start | bytes 393220
  7.6 35.5 %copy-start.5 = (bf16[1,128,512]{2,1,0:T(8,128)(2,1)S(1)}, bf16[1,128,512]{2,1,0:T(8,128)(2,1)}, u32[]{:S(2)}) copy-start(bf16[1,128,512]{2,1,0:T(8,128)(2,1)} %get-tuple-element.44) | copy-start | bytes 393220
  7.6 38.6 %copy-start = (s32[16]{0:T(128)S(1)}, s32[16]{0:T(128)}, u32[]{:S(2)}) copy-start(s32[16]{0:T(128)} %row_shift.3) | copy-start | bytes 196
  7.7 38.6 %copy-start.1 = (s32[16]{0:T(128)S(1)}, s32[16]{0:T(128)}, u32[]{:S(2)}) copy-start(s32[16]{0:T(128)} %frac_index.3) | copy-start | bytes 196
  7.7 21.0 %collective-permute-start.1 = (bf16[2,128,512]{2,1,0:T(8,128)(2,1)S(1)}, bf16[2,128,512]{2,1,0:T(8,128)(2,1)S(1)}, u32[]{:S(2)}, u32[]{:S(2)}) collective-permute-start(bf16[2,128,512]{2,1,0:T(8,128)(2,1)S(1)} %get-tuple-element.82), channel_id=1, source_target_pairs={{0,2},{1,3},{2,0},{3,1},{4,6},{5,7},{6,4},{7,5},{8,10},{9,11},{10,... | collective-permute-start | bytes 786440 | tf_op jit(solution)/shard_map/ppermute | solution.py:382
  7.7 23.6 %collective-permute-start.2 = (bf16[2,128,512]{2,1,0:T(8,128)(2,1)S(1)}, bf16[2,128,512]{2,1,0:T(8,128)(2,1)S(1)}, u32[]{:S(2)}, u32[]{:S(2)}) collective-permute-start(bf16[2,128,512]{2,1,0:T(8,128)(2,1)S(1)} %get-tuple-element.81), channel_id=1, source_target_pairs={{0,3},{1,2},{2,1},{3,0},{4,7},{5,6},{6,5},{7,4},{8,11},{9,10},{10,... | collective-permute-start | bytes 786440 | tf_op jit(solution)/shard_map/ppermute | solution.py:382
  9.2 22.2 %collective-permute-start = (bf16[2,128,512]{2,1,0:T(8,128)(2,1)S(1)}, bf16[2,128,512]{2,1,0:T(8,128)(2,1)S(1)}, u32[]{:S(2)}, u32[]{:S(2)}) collective-permute-start(bf16[2,128,512]{2,1,0:T(8,128)(2,1)S(1)} %get-tuple-element.83), channel_id=1, source_target_pairs={{0,1},{1,0},{2,3},{3,2},{4,5},{5,4},{6,7},{7,6},{8,9},{9,8},{10,11... | collective-permute-start | bytes 786440 | tf_op jit(solution)/shard_map/ppermute | solution.py:382
  10.4 15.4 %collective-permute-start.5 = (bf16[1,128,512]{2,1,0:T(8,128)(2,1)S(1)}, bf16[1,128,512]{2,1,0:T(8,128)(2,1)S(1)}, u32[]{:S(2)}, u32[]{:S(2)}) collective-permute-start(bf16[1,128,512]{2,1,0:T(8,128)(2,1)S(1)} %copy-done.7), channel_id=1, source_target_pairs={{0,5},{1,4},{2,7},{3,6},{4,1},{5,0},{6,3},{7,2},{8,13},{9,12},{10,... | collective-permute-start | bytes 393224 | tf_op jit(solution)/shard_map/ppermute | solution.py:382
  13.5 15.1 %collective-permute-start.3 = (bf16[1,128,512]{2,1,0:T(8,128)(2,1)S(1)}, bf16[1,128,512]{2,1,0:T(8,128)(2,1)S(1)}, u32[]{:S(2)}, u32[]{:S(2)}) collective-permute-start(bf16[1,128,512]{2,1,0:T(8,128)(2,1)S(1)} %copy-done.6), channel_id=1, source_target_pairs={{0,4},{1,5},{2,6},{3,7},{4,0},{5,1},{6,2},{7,3},{8,12},{9,13},{10,... | collective-permute-start | bytes 393224 | tf_op jit(solution)/shard_map/ppermute | solution.py:382
  31.5 11.6 %collective-permute-start.10 = (bf16[1,8,128,128]{3,2,1,0:T(8,128)(2,1)S(1)}, bf16[1,8,128,128]{3,2,1,0:T(8,128)(2,1)S(1)}, u32[]{:S(2)}, u32[]{:S(2)}) collective-permute-start(bf16[1,8,128,128]{3,2,1,0:T(8,128)(2,1)S(1)} %get-tuple-element.42), channel_id=1, source_target_pairs={{0,8},{8,16},{16,24},{1,9},{9,17},{17,25},{2,10},{10,18},{18,26},{... | collective-permute-start | bytes 786440 | tf_op jit(solution)/shard_map/ppermute | solution.py:402
  35.0 8.1 %collective-permute-start.11 = (bf16[1,8,128,128]{3,2,1,0:T(8,128)(2,1)S(1)}, bf16[1,8,128,128]{3,2,1,0:T(8,128)(2,1)S(1)}, u32[]{:S(2)}, u32[]{:S(2)}) collective-permute-start(bf16[1,8,128,128]{3,2,1,0:T(8,128)(2,1)S(1)} %get-tuple-element.43), channel_id=1, source_target_pairs={{8,0},{16,8},{24,16},{9,1},{17,9},{25,17},{10,2},{18,10},{26,18},{... | collective-permute-start | bytes 786440 | tf_op jit(solution)/shard_map/ppermute | solution.py:402
  37.4 17.1 %collective-permute-start.8 = (bf16[1,128,512]{2,1,0:T(8,128)(2,1)S(1)}, bf16[1,128,512]{2,1,0:T(8,128)(2,1)S(1)}, u32[]{:S(2)}, u32[]{:S(2)}) collective-permute-start(bf16[1,128,512]{2,1,0:T(8,128)(2,1)S(1)} %copy-done.4), channel_id=1, source_target_pairs={{0,6},{1,7},{2,4},{3,5},{4,2},{5,3},{6,0},{7,1},{8,14},{9,15},{10,... | collective-permute-start | bytes 393224 | tf_op jit(solution)/shard_map/ppermute | solution.py:382
  40.8 16.1 %collective-permute-start.6 = (bf16[1,128,512]{2,1,0:T(8,128)(2,1)S(1)}, bf16[1,128,512]{2,1,0:T(8,128)(2,1)S(1)}, u32[]{:S(2)}, u32[]{:S(2)}) collective-permute-start(bf16[1,128,512]{2,1,0:T(8,128)(2,1)S(1)} %copy-done.3), channel_id=1, source_target_pairs={{0,5},{1,4},{2,7},{3,6},{4,1},{5,0},{6,3},{7,2},{8,13},{9,12},{10,... | collective-permute-start | bytes 393224 | tf_op jit(solution)/shard_map/ppermute | solution.py:382
  40.8 19.0 %collective-permute-start.4 = (bf16[1,128,512]{2,1,0:T(8,128)(2,1)S(1)}, bf16[1,128,512]{2,1,0:T(8,128)(2,1)S(1)}, u32[]{:S(2)}, u32[]{:S(2)}) collective-permute-start(bf16[1,128,512]{2,1,0:T(8,128)(2,1)S(1)} %get-tuple-element.39), channel_id=1, source_target_pairs={{0,4},{1,5},{2,6},{3,7},{4,0},{5,1},{6,2},{7,3},{8,12},{9,13},{10,... | collective-permute-start | bytes 393224 | tf_op jit(solution)/shard_map/ppermute | solution.py:382
  43.1 11.4 %collective-permute-start.12 = (bf16[1,128,512]{2,1,0:T(8,128)(2,1)S(1)}, bf16[1,128,512]{2,1,0:T(8,128)(2,1)S(1)}, u32[]{:S(2)}, u32[]{:S(2)}) collective-permute-start(bf16[1,128,512]{2,1,0:T(8,128)(2,1)S(1)} %copy-done.5), channel_id=1, source_target_pairs={{0,7},{1,6},{2,5},{3,4},{4,3},{5,2},{6,1},{7,0},{8,15},{9,14},{10,... | collective-permute-start | bytes 393224 | tf_op jit(solution)/shard_map/ppermute | solution.py:382
  59.9 12.7 %collective-permute-start.13 = (bf16[1,8,128,128]{3,2,1,0:T(8,128)(2,1)S(1)}, bf16[1,8,128,128]{3,2,1,0:T(8,128)(2,1)S(1)}, u32[]{:S(2)}, u32[]{:S(2)}) collective-permute-start(bf16[1,8,128,128]{3,2,1,0:T(8,128)(2,1)S(1)} %get-tuple-element.51), channel_id=1, source_target_pairs={{0,8},{8,16},{16,24},{1,9},{9,17},{17,25},{2,10},{10,18},{18,26},{... | collective-permute-start | bytes 786440 | tf_op jit(solution)/shard_map/ppermute | solution.py:402
  64.0 8.7 %collective-permute-start.14 = (bf16[1,8,128,128]{3,2,1,0:T(8,128)(2,1)S(1)}, bf16[1,8,128,128]{3,2,1,0:T(8,128)(2,1)S(1)}, u32[]{:S(2)}, u32[]{:S(2)}) collective-permute-start(bf16[1,8,128,128]{3,2,1,0:T(8,128)(2,1)S(1)} %get-tuple-element.52), channel_id=1, source_target_pairs={{8,0},{16,8},{24,16},{9,1},{17,9},{25,17},{10,2},{18,10},{26,18},{... | collective-permute-start | bytes 786440 | tf_op jit(solution)/shard_map/ppermute | solution.py:402
  65.9 11.4 %collective-permute-start.24 = (bf16[1,128,512]{2,1,0:T(8,128)(2,1)S(1)}, bf16[1,128,512]{2,1,0:T(8,128)(2,1)S(1)}, u32[]{:S(2)}, u32[]{:S(2)}) collective-permute-start(bf16[1,128,512]{2,1,0:T(8,128)(2,1)S(1)} %get-tuple-element.61), channel_id=1, source_target_pairs={{0,1},{1,0},{2,9},{3,8},{4,17},{5,16},{6,25},{7,24},{8,5},{9,4},{1... | collective-permute-start | bytes 393224 | tf_op jit(solution)/shard_map/ppermute | solution.py:422
  67.1 23.3 %collective-permute-start.23 = (bf16[1,128,512]{2,1,0:T(8,128)(2,1)S(1)}, bf16[1,128,512]{2,1,0:T(8,128)(2,1)S(1)}, u32[]{:S(2)}, u32[]{:S(2)}) collective-permute-start(bf16[1,128,512]{2,1,0:T(8,128)(2,1)S(1)} %get-tuple-element.49), channel_id=1, source_target_pairs={{0,0},{1,1},{2,8},{3,9},{4,16},{5,17},{6,24},{7,25},{8,4},{9,5},{1... | collective-permute-start | bytes 393224 | tf_op jit(solution)/shard_map/ppermute | solution.py:422
  72.2 16.2 %collective-permute-start.25 = (bf16[1,128,512]{2,1,0:T(8,128)(2,1)S(1)}, bf16[1,128,512]{2,1,0:T(8,128)(2,1)S(1)}, u32[]{:S(2)}, u32[]{:S(2)}) collective-permute-start(bf16[1,128,512]{2,1,0:T(8,128)(2,1)S(1)} %get-tuple-element.62), channel_id=1, source_target_pairs={{0,2},{1,3},{2,10},{3,11},{4,18},{5,19},{6,26},{7,27},{8,6},{9,7},... | collective-permute-start | bytes 393224 | tf_op jit(solution)/shard_map/ppermute | solution.py:422
  72.7 22.2 %collective-permute-start.26 = (bf16[1,128,512]{2,1,0:T(8,128)(2,1)S(1)}, bf16[1,128,512]{2,1,0:T(8,128)(2,1)S(1)}, u32[]{:S(2)}, u32[]{:S(2)}) collective-permute-start(bf16[1,128,512]{2,1,0:T(8,128)(2,1)S(1)} %get-tuple-element.64), channel_id=1, source_target_pairs={{0,3},{1,2},{2,11},{3,10},{4,19},{5,18},{6,27},{7,26},{8,7},{9,6},... | collective-permute-start | bytes 393224 | tf_op jit(solution)/shard_map/ppermute | solution.py:422
  77.3 19.5 %collective-permute-start.27 = (bf16[1,128,512]{2,1,0:T(8,128)(2,1)S(1)}, bf16[1,128,512]{2,1,0:T(8,128)(2,1)S(1)}, u32[]{:S(2)}, u32[]{:S(2)}) collective-permute-start(bf16[1,128,512]{2,1,0:T(8,128)(2,1)S(1)} %get-tuple-element.66), channel_id=1, source_target_pairs={{0,4},{1,5},{2,12},{3,13},{4,20},{5,21},{6,28},{7,29},{8,0},{9,1},... | collective-permute-start | bytes 393224 | tf_op jit(solution)/shard_map/ppermute | solution.py:422
  77.3 20.8 %collective-permute-start.28 = (bf16[1,128,512]{2,1,0:T(8,128)(2,1)S(1)}, bf16[1,128,512]{2,1,0:T(8,128)(2,1)S(1)}, u32[]{:S(2)}, u32[]{:S(2)}) collective-permute-start(bf16[1,128,512]{2,1,0:T(8,128)(2,1)S(1)} %get-tuple-element.68), channel_id=1, source_target_pairs={{0,5},{1,4},{2,13},{3,12},{4,21},{5,20},{6,29},{7,28},{8,1},{9,0},... | collective-permute-start | bytes 393224 | tf_op jit(solution)/shard_map/ppermute | solution.py:422
  88.4 13.0 %collective-permute-start.29 = (bf16[1,128,512]{2,1,0:T(8,128)(2,1)S(1)}, bf16[1,128,512]{2,1,0:T(8,128)(2,1)S(1)}, u32[]{:S(2)}, u32[]{:S(2)}) collective-permute-start(bf16[1,128,512]{2,1,0:T(8,128)(2,1)S(1)} %get-tuple-element.70), channel_id=1, source_target_pairs={{0,6},{1,7},{2,14},{3,15},{4,22},{5,23},{6,30},{7,31},{8,2},{9,3},... | collective-permute-start | bytes 393224 | tf_op jit(solution)/shard_map/ppermute | solution.py:422
  90.4 12.7 %collective-permute-start.30 = (bf16[1,128,512]{2,1,0:T(8,128)(2,1)S(1)}, bf16[1,128,512]{2,1,0:T(8,128)(2,1)S(1)}, u32[]{:S(2)}, u32[]{:S(2)}) collective-permute-start(bf16[1,128,512]{2,1,0:T(8,128)(2,1)S(1)} %get-tuple-element.72), channel_id=1, source_target_pairs={{0,7},{1,6},{2,15},{3,14},{4,23},{5,22},{6,31},{7,30},{8,3},{9,2},... | collective-permute-start | bytes 393224 | tf_op jit(solution)/shard_map/ppermute | solution.py:422
  94.9 11.1 %collective-permute-start.15 = (bf16[1,128,512]{2,1,0:T(8,128)(2,1)S(1)}, bf16[1,128,512]{2,1,0:T(8,128)(2,1)S(1)}, u32[]{:S(2)}, u32[]{:S(2)}) collective-permute-start(bf16[1,128,512]{2,1,0:T(8,128)(2,1)S(1)} %get-tuple-element.53), channel_id=1, source_target_pairs={{0,0},{1,1},{2,8},{3,9},{4,16},{5,17},{6,24},{7,25},{8,4},{9,5},{1... | collective-permute-start | bytes 393224 | tf_op jit(solution)/shard_map/ppermute | solution.py:422
  96.8 17.6 %collective-permute-start.16 = (bf16[1,128,512]{2,1,0:T(8,128)(2,1)S(1)}, bf16[1,128,512]{2,1,0:T(8,128)(2,1)S(1)}, u32[]{:S(2)}, u32[]{:S(2)}) collective-permute-start(bf16[1,128,512]{2,1,0:T(8,128)(2,1)S(1)} %get-tuple-element.54), channel_id=1, source_target_pairs={{0,1},{1,0},{2,9},{3,8},{4,17},{5,16},{6,25},{7,24},{8,5},{9,4},{1... | collective-permute-start | bytes 393224 | tf_op jit(solution)/shard_map/ppermute | solution.py:422
  98.1 18.2 %collective-permute-start.17 = (bf16[1,128,512]{2,1,0:T(8,128)(2,1)S(1)}, bf16[1,128,512]{2,1,0:T(8,128)(2,1)S(1)}, u32[]{:S(2)}, u32[]{:S(2)}) collective-permute-start(bf16[1,128,512]{2,1,0:T(8,128)(2,1)S(1)} %get-tuple-element.55), channel_id=1, source_target_pairs={{0,2},{1,3},{2,10},{3,11},{4,18},{5,19},{6,26},{7,27},{8,6},{9,7},... | collective-permute-start | bytes 393224 | tf_op jit(solution)/shard_map/ppermute | solution.py:422
  101.5 17.2 %collective-permute-start.18 = (bf16[1,128,512]{2,1,0:T(8,128)(2,1)S(1)}, bf16[1,128,512]{2,1,0:T(8,128)(2,1)S(1)}, u32[]{:S(2)}, u32[]{:S(2)}) collective-permute-start(bf16[1,128,512]{2,1,0:T(8,128)(2,1)S(1)} %get-tuple-element.56), channel_id=1, source_target_pairs={{0,3},{1,2},{2,11},{3,10},{4,19},{5,18},{6,27},{7,26},{8,7},{9,6},... | collective-permute-start | bytes 393224 | tf_op jit(solution)/shard_map/ppermute | solution.py:422
  103.1 15.6 %collective-permute-start.19 = (bf16[1,128,512]{2,1,0:T(8,128)(2,1)S(1)}, bf16[1,128,512]{2,1,0:T(8,128)(2,1)S(1)}, u32[]{:S(2)}, u32[]{:S(2)}) collective-permute-start(bf16[1,128,512]{2,1,0:T(8,128)(2,1)S(1)} %get-tuple-element.57), channel_id=1, source_target_pairs={{0,4},{1,5},{2,12},{3,13},{4,20},{5,21},{6,28},{7,29},{8,0},{9,1},... | collective-permute-start | bytes 393224 | tf_op jit(solution)/shard_map/ppermute | solution.py:422
  106.0 12.7 %collective-permute-start.20 = (bf16[1,128,512]{2,1,0:T(8,128)(2,1)S(1)}, bf16[1,128,512]{2,1,0:T(8,128)(2,1)S(1)}, u32[]{:S(2)}, u32[]{:S(2)}) collective-permute-start(bf16[1,128,512]{2,1,0:T(8,128)(2,1)S(1)} %get-tuple-element.58), channel_id=1, source_target_pairs={{0,5},{1,4},{2,13},{3,12},{4,21},{5,20},{6,29},{7,28},{8,1},{9,0},... | collective-permute-start | bytes 393224 | tf_op jit(solution)/shard_map/ppermute | solution.py:422
  114.4 9.8 %collective-permute-start.21 = (bf16[1,128,512]{2,1,0:T(8,128)(2,1)S(1)}, bf16[1,128,512]{2,1,0:T(8,128)(2,1)S(1)}, u32[]{:S(2)}, u32[]{:S(2)}) collective-permute-start(bf16[1,128,512]{2,1,0:T(8,128)(2,1)S(1)} %get-tuple-element.59), channel_id=1, source_target_pairs={{0,6},{1,7},{2,14},{3,15},{4,22},{5,23},{6,30},{7,31},{8,2},{9,3},... | collective-permute-start | bytes 393224 | tf_op jit(solution)/shard_map/ppermute | solution.py:422
  116.3 9.3 %collective-permute-start.22 = (bf16[1,128,512]{2,1,0:T(8,128)(2,1)S(1)}, bf16[1,128,512]{2,1,0:T(8,128)(2,1)S(1)}, u32[]{:S(2)}, u32[]{:S(2)}) collective-permute-start(bf16[1,128,512]{2,1,0:T(8,128)(2,1)S(1)} %get-tuple-element.60), channel_id=1, source_target_pairs={{0,7},{1,6},{2,15},{3,14},{4,23},{5,22},{6,31},{7,30},{8,3},{9,2},... | collective-permute-start | bytes 393224 | tf_op jit(solution)/shard_map/ppermute | solution.py:422
